TPU v7x, 32 devices: a whole 2x2x4 slice. The times are simulated.
32 devices in a mesh: grp: 2 (over x), gx: 16 (over z, y, core).
Axes of the slice: x: 2, y: 2, z: 4, core: 2. Of those that a mesh axis runs over, the one named last changes fastest.
Arguments:
- state_field: float32 [32, 20, 16, 512], P(('grp', 'gx')), parts along dimension 0, may hold values from -6 to 6
- cotangent: float32 [32, 20, 16, 512], P(('grp', 'gx')), parts along dimension 0, may hold values from -6 to 6
- spec_weight: float32 [192, 12, 12, 2, 20, 20], P('gx'), may hold values from -2.5 to 2.5
- point_weight: float32 [20, 20], replicated, may hold values from -1.25 to 1.25
- bias_vector: float32 [20], replicated, may hold values from -3 to 3
Outputs:
- layer_out: float32 [32, 20, 16, 512], P(('grp', 'gx')), parts along dimension 0
- field_grad: float32 [32, 20, 16, 512], P(('grp', 'gx')), parts along dimension 0
- spec_grad: float32 [384, 12, 12, 2, 20, 20], P(('grp', 'gx')), parts along dimension 0
- point_grad: float32 [40, 20], P('grp'), parts along dimension 0
- bias_grad: float32 [40], P('grp'), parts along dimension 0
There are 2 independent parts, one for each index of `grp`. A program takes and returns all parts, laid end to end along the dimension named above; an argument that names none is the same for every part. Nothing has to cross between parts.
All inputs are finite; a program needn't handle non-finite values.
Results may differ from a plain program's by a relative error of at most 0.00011.
Values sent between devices are 32-bit elements; how exact they have to be, the bound alone decides.
A program may use at most 320 MiB of HBM per device.

v0:
```python
import math

import jax
import jax.numpy as jnp
from jax import lax
from jax.sharding import PartitionSpec as P

MX = 12
MY = 12
MZ = 24
MT = 8
NZ = 32
NT = 16


precise = lax.Precision.HIGHEST


def waves(count, length):
    modes = jnp.arange(count, dtype=jnp.int32)
    freqs = jnp.where(modes < count // 2, modes, modes - count)
    places = jnp.arange(length, dtype=jnp.int32)
    phase = jnp.remainder(freqs[:, None] * places[None, :], length)
    angle = 2.0 * math.pi / length * phase.astype(jnp.float32)
    return (jnp.cos(angle), jnp.sin(angle))


def depth_time(norm_scale, doubled):
    modes = jnp.arange(MZ * MT, dtype=jnp.int32)
    depth_mode = modes // MT
    time_mode = modes % MT
    depth_freq = jnp.where(depth_mode < MZ // 2, depth_mode, depth_mode - MZ)
    cells = jnp.arange(NZ * NT, dtype=jnp.int32)
    depth_pos = cells // NT
    time_pos = cells % NT
    phase = (
        depth_freq[:, None] * depth_pos[None, :] * NT + time_mode[:, None] * time_pos[None, :] * NZ
    )
    phase = jnp.remainder(phase, NZ * NT)
    angle = 2.0 * math.pi / (NZ * NT) * phase.astype(jnp.float32)
    factor = jnp.full((MZ * MT,), norm_scale, jnp.float32)
    if doubled:
        factor = factor * jnp.where(time_mode == 0, 1.0, 2.0).astype(jnp.float32)
    return jnp.stack([factor[:, None] * jnp.cos(angle), -factor[:, None] * jnp.sin(angle)])


def complex_apply(packed, cos_table, sin_table, target, sign):
    real_part = packed[:, :, 0]
    imag_part = packed[:, :, 1]
    position = target if target < 2 else target - 1

    def contract(wave_table, operand):
        product = jnp.tensordot(wave_table, operand, axes=((1,), (position,)), precision=precise)
        return jnp.moveaxis(product, 0, position)

    new_real = contract(cos_table, real_part) - sign * contract(sin_table, imag_part)
    new_imag = contract(cos_table, imag_part) + sign * contract(sin_table, real_part)
    return jnp.stack([new_real, new_imag], axis=2)


def mult(form, left, right):
    return jnp.einsum(form, left, right, precision=precise)


def local(state_field, cotangent, spec_weight, point_weight, bias_vector):
    rows_x = state_field.shape[0]
    full_x = rows_x * lax.axis_size("gx")
    rows_y = state_field.shape[2]
    norm_scale = float(full_x * rows_y * NZ * NT) ** (-0.5)
    x_cos, x_sin = waves(MX, full_x)
    y_cos, y_sin = waves(MY, rows_y)
    plain_table = depth_time(norm_scale, False)
    double_table = depth_time(norm_scale, True)

    def to_modes(grid_values, lift_table):
        lifted = jnp.einsum("xcyn,pmn->xcpym", grid_values, lift_table, precision=precise)
        lifted = complex_apply(lifted, y_cos, y_sin, 3, -1.0)

        def finish_grid(piece):
            return complex_apply(piece, x_cos, x_sin, 0, -1.0)

        return finish_grid(lax.all_to_all(lifted, "gx", split_axis=4, concat_axis=0, tiled=True))

    def to_grid(modes_values, lower_table):
        spread = complex_apply(modes_values, x_cos.T, x_sin.T, 0, 1.0)

        def finish_grid(piece):
            along_y = complex_apply(piece, y_cos.T, y_sin.T, 3, 1.0)
            return jnp.einsum("xcpym,pmn->xcyn", along_y, lower_table, precision=precise)

        return finish_grid(lax.all_to_all(spread, "gx", split_axis=0, concat_axis=4, tiled=True))

    spectrum = to_modes(state_field, plain_table)
    spec_real = spectrum[:, :, 0]
    spec_imag = spectrum[:, :, 1]
    weight_real = spec_weight[:, :, :, 0]
    weight_imag = spec_weight[:, :, :, 1]
    mixed_real = mult("kyxio,xiyk->xoyk", weight_real, spec_real) - mult(
        "kyxio,xiyk->xoyk", weight_imag, spec_imag
    )
    mixed_imag = mult("kyxio,xiyk->xoyk", weight_real, spec_imag) + mult(
        "kyxio,xiyk->xoyk", weight_imag, spec_real
    )
    spectral = to_grid(jnp.stack([mixed_real, mixed_imag], axis=2), double_table)
    local_part = mult("xiyn,io->xoyn", state_field, point_weight)
    pre = spectral + local_part + bias_vector[None, :, None, None]
    layer_out = jax.nn.gelu(pre, approximate=False)
    cumulative = 0.5 * (1.0 + jax.scipy.special.erf(pre * (1.0 / math.sqrt(2.0))))
    density = jnp.exp(-0.5 * pre * pre) * (1.0 / math.sqrt(2.0 * math.pi))
    dpre = cotangent * (cumulative + pre * density)
    point_local = mult("xiyn,xoyn->io", state_field, dpre)
    bias_local = jnp.sum(dpre, axis=(0, 2, 3))
    point_total, bias_total = lax.psum((point_local, bias_local), "gx")
    back_modes = to_modes(dpre, double_table)
    back_real = back_modes[:, :, 0]
    back_imag = back_modes[:, :, 1]
    input_real = mult("kyxio,xoyk->xiyk", weight_real, back_real) + mult(
        "kyxio,xoyk->xiyk", weight_imag, back_imag
    )
    input_imag = mult("kyxio,xoyk->xiyk", weight_real, back_imag) - mult(
        "kyxio,xoyk->xiyk", weight_imag, back_real
    )
    grad_real = mult("xiyk,xoyk->kyxio", spec_real, back_real) + mult(
        "xiyk,xoyk->kyxio", spec_imag, back_imag
    )
    grad_imag = mult("xiyk,xoyk->kyxio", spec_real, back_imag) - mult(
        "xiyk,xoyk->kyxio", spec_imag, back_real
    )
    spec_grad = jnp.stack([grad_real, grad_imag], axis=3)
    field_spectral = to_grid(jnp.stack([input_real, input_imag], axis=2), plain_table)
    field_grad = field_spectral + mult("xoyn,io->xiyn", dpre, point_weight)
    return (layer_out, field_grad, spec_grad, point_total * norm_scale, bias_total * norm_scale)


def solution(mesh):
    in_specs = (
        P(("grp", "gx"), None, None, None),
        P(("grp", "gx"), None, None, None),
        P("gx", None, None, None, None, None),
        P(),
        P(),
    )
    out_specs = (
        P(("grp", "gx"), None, None, None),
        P(("grp", "gx"), None, None, None),
        P(("grp", "gx"), None, None, None, None, None),
        P("grp", None),
        P("grp"),
    )
    return jax.shard_map(local, mesh=mesh, in_specs=in_specs, out_specs=out_specs, check_vma=False)
```

profile of v0, /device:TPU:0, one launch (start us, length us, event | category | flops | bytes accessed | tf_op | source)
XLA Modules:
  0.0 626.1 jit_solution(14339088784563132028)
XLA Ops:
  8.3 8.5 %copy.170 = f32[1,20,2,12,192]{1,2,3,0,4:T(2,128)S(1)} copy(f32[1,20,2,12,192]{4,3,1,2,0:T(8,128)} %pad_maximum_fusion.3) | data formatting | bytes 737280 | tf_op jit(solution)/shard_map/stack | solution.py:58
  16.8 4.9 reshape.744
  21.7 7.7 %all-to-all-start = ((f32[16,1,5760]{2,1,0:T(1,128)}), f32[16,1,5760]{2,1,0:T(1,128)S(1)}, u32[]{:S(2)}, u32[]{:S(2)}) async-start(f32[16,1,5760]{2,1,0:T(1,128)} %reshape.744), calls=%async_computation | async-start | bytes 737280 | tf_op jit(solution)/shard_map/all_to_all | solution.py:82
  29.4 37.5 %fusion.338 = (f32[12,12,12,1,20,20]{5,3,4,2,1,0:T(1,128)}, f32[12,12,12,1,20,20]{5,3,4,2,1,0:T(1,128)}) fusion(f32[12,12,12,2,20,20]{5,3,4,2,1,0:T(2,128)} %param.7), kind=kLoop, calls=%fused_computation.391 | loop fusion | bytes 11059200 | tf_op jit(solution)/shard_map/slice | solution.py:96
  68.9 3.9 reshape.745
  79.2 24.0 %fusion.16 = f32[12,12,12,1,20]{4,3,2,1,0:T(1,128)} fusion(f32[12,12,12,1,20,20]{5,3,4,2,1,0:T(1,128)} %get-tuple-element.29, f32[12,20,12,12,1]{1,0,3,2,4:T(8,128)S(1)} %bitcast.444), kind=kOutput, calls=%fused_computation.17 | convolution fusion | flops 8294400 | bytes 3041280 | tf_op jit(solution)/shard_map/kyxio,xiyk->xoyk/dot_general | solution.py:62
  103.2 20.8 %fusion.18 = f32[12,12,12,1,20]{4,3,2,1,0:T(1,128)} fusion(f32[12,12,12,1,20,20]{5,3,4,2,1,0:T(1,128)S(1)} %bitcast.426, f32[12,20,12,12,1]{1,0,3,2,4:T(8,128)S(1)} %bitcast.446), kind=kOutput, calls=%fused_computation.19 | convolution fusion | flops 8294400 | bytes 3041280 | tf_op jit(solution)/shard_map/kyxio,xiyk->xoyk/dot_general | solution.py:62
  124.1 20.2 %fusion.4 = f32[12,12,12,1,20]{4,3,2,1,0:T(1,128)S(1)} fusion(f32[12,12,12,1,20,20]{5,3,4,2,1,0:T(1,128)S(1)} %bitcast.430, f32[12,20,12,12,1]{1,0,3,2,4:T(8,128)S(1)} %bitcast.447), kind=kOutput, calls=%fused_computation.5 | convolution fusion | flops 8294400 | bytes 3041280 | tf_op jit(solution)/shard_map/kyxio,xiyk->xoyk/dot_general | solution.py:62
  144.3 20.7 %fusion.6 = f32[12,12,12,1,20]{4,3,2,1,0:T(1,128)S(1)} fusion(f32[12,12,12,1,20,20]{5,3,4,2,1,0:T(1,128)S(1)} %bitcast.430, f32[12,20,12,12,1]{1,0,3,2,4:T(8,128)S(1)} %bitcast.445), kind=kOutput, calls=%fused_computation.7 | convolution fusion | flops 8294400 | bytes 3041280 | tf_op jit(solution)/shard_map/kyxio,xiyk->xoyk/dot_general | solution.py:62
  175.0 5.6 reshape.746
  180.6 6.1 all-to-all-start.1
  188.8 9.7 %all-to-all-done.1 = f32[16,1,5760]{2,1,0:T(1,128)S(1)} async-done(((f32[16,1,5760]{2,1,0:T(1,128)}), f32[16,1,5760]{2,1,0:T(1,128)S(1)}, u32[]{:S(2)}, u32[]{:S(2)}) %all-to-all-start.1) | async-done | bytes 368672 | tf_op jit(solution)/shard_map/all_to_all | solution.py:91
  200.8 6.3 %reshape.747 = f32[16,12,12,2,20]{4,3,2,1,0:T(2,128)} reshape(f32[16,5760]{1,0:T(8,128)} %reduce.1) | data formatting | bytes 737280
  207.1 3.9 bitcast_bitcast_fusion.1
  211.0 7.1 %copy.272 = f32[1,20,2,12,16,12]{5,4,3,1,2,0:T(8,128)} copy(f32[1,20,2,12,16,12]{1,2,5,3,4,0:T(2,128)} %bitcast_bitcast_fusion.1) | data formatting | bytes 737280 | tf_op jit(solution)/shard_map/all_to_all | solution.py:91
  218.0 4.4 reshape.742
  234.6 59.8 %all-reduce = (f32[20,20]{0,1:T(8,128)S(1)}, f32[20]{0:T(128)S(1)}) all-reduce(f32[20,20]{0,1:T(8,128)S(1)} %convolution_bitcast_fusion.4, f32[20]{0:T(128)S(1)} %get-tuple-element.27), channel_id=1, replica_groups=mesh['grp'=2,'gx'=16] {'gx'}, use_global_device_ids=true, to_apply=%region_0.1 | all-reduce | flops 420 | bytes 3360 | tf_op jit(solution)/shard_map/psum | solution.py:113
  300.5 5.5 reshape.748
  306.0 4.0 all-to-all-start.2
  312.8 9.0 %all-to-all-done.2 = f32[16,1,5760]{2,1,0:T(1,128)S(1)} async-done(((f32[16,1,5760]{2,1,0:T(1,128)}), f32[16,1,5760]{2,1,0:T(1,128)S(1)}, u32[]{:S(2)}, u32[]{:S(2)}) %all-to-all-start.2) | async-done | bytes 368672 | tf_op jit(solution)/shard_map/all_to_all | solution.py:82
  323.3 5.3 reshape.749
  334.3 37.5 %fusion.12 = f32[12,12,12,1,20]{4,3,2,1,0:T(1,128)} fusion(f32[12,12,12,1,20,20]{5,3,4,2,1,0:T(1,128)} %get-tuple-element.29, f32[12,20,12,12,1]{1,0,3,2,4:T(8,128)S(1)} %bitcast.448), kind=kOutput, calls=%fused_computation.13 | convolution fusion | flops 8294400 | bytes 3041280 | tf_op jit(solution)/shard_map/kyxio,xoyk->xiyk/dot_general | solution.py:62
  371.9 34.6 %fusion.2 = f32[12,12,12,1,20]{4,3,2,1,0:T(1,128)} fusion(f32[12,12,12,1,20,20]{5,3,4,2,1,0:T(1,128)S(1)} %bitcast.432, f32[12,20,12,12,1]{1,0,3,2,4:T(8,128)S(1)} %bitcast.449), kind=kOutput, calls=%fused_computation.3 | convolution fusion | flops 8294400 | bytes 3041280 | tf_op jit(solution)/shard_map/kyxio,xoyk->xiyk/dot_general | solution.py:62
  410.0 35.2 %fusion = f32[12,12,12,1,20]{4,3,2,1,0:T(1,128)} fusion(f32[12,12,12,1,20,20]{5,3,4,2,1,0:T(1,128)S(1)} %bitcast.432, f32[12,20,12,12,1]{1,0,3,2,4:T(8,128)} %bitcast.450), kind=kOutput, calls=%fused_computation.1 | convolution fusion | flops 8294400 | bytes 3041280 | tf_op jit(solution)/shard_map/kyxio,xoyk->xiyk/dot_general | solution.py:62
  445.3 34.6 %fusion.14 = f32[12,12,12,1,20]{4,3,2,1,0:T(1,128)S(1)} fusion(f32[12,12,12,1,20,20]{5,3,4,2,1,0:T(1,128)S(1)} %bitcast.428, f32[12,20,12,12,1]{1,0,3,2,4:T(8,128)} %bitcast.451), kind=kOutput, calls=%fused_computation.15 | convolution fusion | flops 8294400 | bytes 3041280 | tf_op jit(solution)/shard_map/kyxio,xoyk->xiyk/dot_general | solution.py:62
  479.9 17.1 %add_bitcast_fusion = (f32[12,12,12,1,20,20]{5,4,2,1,0,3:T(8,128)}, f32[12,12,12,1,20,20]{5,4,2,1,0,3:T(8,128)}) fusion(f32[12,20,12,12]{1,0,3,2:T(8,128)S(1)} %fusion.31, f32[12,20,12,12]{1,0,3,2:T(8,128)S(1)} %copy-done.4, f32[12,20,12,12]{1,0,3,2:T(8,128)S(1)} %fusion.30, f32[12,20,12,12]{1,0,3,2:T(8,128)S(1)} %copy-done.3), kind=kLoop, calls=%fused_computation.26 | loop fusion | flops 4147200 | bytes 6082560 | tf_op jit(solution)/shard_map/stack | solution.py:129
  505.8 4.9 reshape.750
  510.6 3.8 all-to-all-start.3
  514.4 30.4 %pad_maximum_fusion = f32[12,12,12,2,20,20]{5,4,2,1,0,3:T(8,128)} fusion(f32[12,12,12,1,20,20]{5,4,2,1,0,3:T(8,128)} %get-tuple-element.32, f32[12,12,12,1,20,20]{5,4,2,1,0,3:T(8,128)} %get-tuple-element.31), kind=kLoop, calls=%fused_computation | loop fusion | flops 1382400 | bytes 11059200 | tf_op jit(solution)/shard_map/stack | solution.py:129
  544.8 58.2 %copy.214 = f32[12,12,12,2,20,20]{5,3,4,2,1,0:T(2,128)} copy(f32[12,12,12,2,20,20]{5,4,2,1,0,3:T(8,128)} %pad_maximum_fusion) | data formatting | bytes 11059200
  604.6 5.3 reshape.751
  612.4 5.5 copy.274
  (158 shorter events, 82.3 us)
Async XLA Ops:
  0.6 186.1 %copy-start = (f32[20,20]{1,0:T(8,128)S(1)}, f32[20,20]{1,0:T(8,128)}, u32[]{:S(2)}) copy-start(f32[20,20]{1,0:T(8,128)} %param.8) | copy-start | bytes 4804
  21.7 45.1 %all-to-all-start = ((f32[16,1,5760]{2,1,0:T(1,128)}), f32[16,1,5760]{2,1,0:T(1,128)S(1)}, u32[]{:S(2)}, u32[]{:S(2)}) async-start(f32[16,1,5760]{2,1,0:T(1,128)} %reshape.744), calls=%async_computation | async-start | bytes 737280 | tf_op jit(solution)/shard_map/all_to_all | solution.py:82
  75.4 27.8 %slice-start = ((s8[17694720]{0:T(1024)(128)(4,1)}), s8[4194304]{0:T(1024)(128)(4,1)S(1)}, s32[]{:S(2)}) async-start(s8[17694720]{0:T(1024)(128)(4,1)} %bitcast.425), calls=%async_computation.4 | async-start | bytes 8388608
  77.9 25.3 %slice-start.1 = ((s8[17694720]{0:T(1024)(128)(4,1)}), s8[4194304]{0:T(1024)(128)(4,1)S(1)}, s32[]{:S(2)}) async-start(s8[17694720]{0:T(1024)(128)(4,1)} %bitcast.425), calls=%async_computation.5 | async-start | bytes 8388608
  79.1 24.1 %slice-start.2 = ((s8[17694720]{0:T(1024)(128)(4,1)}), s8[4194304]{0:T(1024)(128)(4,1)S(1)}, s32[]{:S(2)}) async-start(s8[17694720]{0:T(1024)(128)(4,1)} %bitcast.425), calls=%async_computation.6 | async-start | bytes 8388608
  79.2 24.0 %slice-start.3 = ((s8[17694720]{0:T(1024)(128)(4,1)}), s8[4194304]{0:T(1024)(128)(4,1)S(1)}, s32[]{:S(2)}) async-start(s8[17694720]{0:T(1024)(128)(4,1)} %bitcast.425), calls=%async_computation.7 | async-start | bytes 8388608
  79.2 24.0 %slice-start.4 = ((s8[17694720]{0:T(1024)(128)(4,1)}), s8[917504]{0:T(1024)(128)(4,1)S(1)}, s32[]{:S(2)}) async-start(s8[17694720]{0:T(1024)(128)(4,1)} %bitcast.425), calls=%async_computation.8 | async-start | bytes 1835008
  79.2 44.9 %slice-start.10 = ((s8[17694720]{0:T(1024)(128)(4,1)}), s8[4194304]{0:T(1024)(128)(4,1)S(1)}, s32[]{:S(2)}) async-start(s8[17694720]{0:T(1024)(128)(4,1)} %bitcast.429), calls=%async_computation.14 | async-start | bytes 8388608
  79.2 44.9 %slice-start.11 = ((s8[17694720]{0:T(1024)(128)(4,1)}), s8[4194304]{0:T(1024)(128)(4,1)S(1)}, s32[]{:S(2)}) async-start(s8[17694720]{0:T(1024)(128)(4,1)} %bitcast.429), calls=%async_computation.15 | async-start | bytes 8388608
  79.2 44.9 %slice-start.12 = ((s8[17694720]{0:T(1024)(128)(4,1)}), s8[4194304]{0:T(1024)(128)(4,1)S(1)}, s32[]{:S(2)}) async-start(s8[17694720]{0:T(1024)(128)(4,1)} %bitcast.429), calls=%async_computation.16 | async-start | bytes 8388608
  103.2 20.9 %slice-start.13 = ((s8[17694720]{0:T(1024)(128)(4,1)}), s8[4194304]{0:T(1024)(128)(4,1)S(1)}, s32[]{:S(2)}) async-start(s8[17694720]{0:T(1024)(128)(4,1)} %bitcast.429), calls=%async_computation.17 | async-start | bytes 8388608
  103.2 20.9 %slice-start.14 = ((s8[17694720]{0:T(1024)(128)(4,1)}), s8[917504]{0:T(1024)(128)(4,1)S(1)}, s32[]{:S(2)}) async-start(s8[17694720]{0:T(1024)(128)(4,1)} %bitcast.429), calls=%async_computation.18 | async-start | bytes 1835008
  144.3 20.7 %copy-start.8 = (f32[12,12,12,1,20]{4,3,2,1,0:T(1,128)S(1)}, f32[12,12,12,1,20]{4,3,2,1,0:T(1,128)}, u32[]{:S(2)}) copy-start(f32[12,12,12,1,20]{4,3,2,1,0:T(1,128)} %fusion.18) | copy-start | bytes 414724
  180.6 17.9 %all-to-all-start.1 = ((f32[16,1,5760]{2,1,0:T(1,128)}), f32[16,1,5760]{2,1,0:T(1,128)S(1)}, u32[]{:S(2)}, u32[]{:S(2)}) async-start(f32[16,1,5760]{2,1,0:T(1,128)} %reshape.746), calls=%async_computation.1 | async-start | bytes 737280 | tf_op jit(solution)/shard_map/all_to_all | solution.py:91
  222.4 3.2 copy-start.11
  300.5 10.0 %copy-start.20 = (f32[20,16,512]{2,1,0:T(8,128)S(1)}, f32[20,16,512]{2,1,0:T(8,128)}, u32[]{:S(2)}) copy-start(f32[20,16,512]{2,1,0:T(8,128)} %get-tuple-element.41) | copy-start | bytes 1966084
  306.0 15.8 %all-to-all-start.2 = ((f32[16,1,5760]{2,1,0:T(1,128)}), f32[16,1,5760]{2,1,0:T(1,128)S(1)}, u32[]{:S(2)}, u32[]{:S(2)}) async-start(f32[16,1,5760]{2,1,0:T(1,128)} %reshape.748), calls=%async_computation.2 | async-start | bytes 737280 | tf_op jit(solution)/shard_map/all_to_all | solution.py:82
  328.6 43.3 %slice-start.15 = ((s8[17694720]{0:T(1024)(128)(4,1)}), s8[4194304]{0:T(1024)(128)(4,1)S(1)}, s32[]{:S(2)}) async-start(s8[17694720]{0:T(1024)(128)(4,1)} %bitcast.431), calls=%async_computation.19 | async-start | bytes 8388608
  333.0 38.9 %slice-start.16 = ((s8[17694720]{0:T(1024)(128)(4,1)}), s8[4194304]{0:T(1024)(128)(4,1)S(1)}, s32[]{:S(2)}) async-start(s8[17694720]{0:T(1024)(128)(4,1)} %bitcast.431), calls=%async_computation.20 | async-start | bytes 8388608
  334.3 37.6 %copy-start.2 = (f32[12,20,12,12]{1,0,3,2:T(8,128)}, f32[12,20,12,12]{1,0,3,2:T(8,128)S(1)}, u32[]{:S(2)}) copy-start(f32[12,20,12,12]{1,0,3,2:T(8,128)S(1)} %fusion.26) | copy-start | bytes 414724
  334.3 37.6 %slice-start.17 = ((s8[17694720]{0:T(1024)(128)(4,1)}), s8[4194304]{0:T(1024)(128)(4,1)S(1)}, s32[]{:S(2)}) async-start(s8[17694720]{0:T(1024)(128)(4,1)} %bitcast.431), calls=%async_computation.21 | async-start | bytes 8388608
  334.3 37.6 %slice-start.18 = ((s8[17694720]{0:T(1024)(128)(4,1)}), s8[4194304]{0:T(1024)(128)(4,1)S(1)}, s32[]{:S(2)}) async-start(s8[17694720]{0:T(1024)(128)(4,1)} %bitcast.431), calls=%async_computation.22 | async-start | bytes 8388608
  334.3 37.6 %slice-start.19 = ((s8[17694720]{0:T(1024)(128)(4,1)}), s8[917504]{0:T(1024)(128)(4,1)S(1)}, s32[]{:S(2)}) async-start(s8[17694720]{0:T(1024)(128)(4,1)} %bitcast.431), calls=%async_computation.23 | async-start | bytes 1835008
  371.9 73.4 %slice-start.5 = ((s8[17694720]{0:T(1024)(128)(4,1)}), s8[4194304]{0:T(1024)(128)(4,1)S(1)}, s32[]{:S(2)}) async-start(s8[17694720]{0:T(1024)(128)(4,1)} %bitcast.427), calls=%async_computation.9 | async-start | bytes 8388608
  371.9 73.4 %slice-start.6 = ((s8[17694720]{0:T(1024)(128)(4,1)}), s8[4194304]{0:T(1024)(128)(4,1)S(1)}, s32[]{:S(2)}) async-start(s8[17694720]{0:T(1024)(128)(4,1)} %bitcast.427), calls=%async_computation.10 | async-start | bytes 8388608
  371.9 73.3 %slice-start.7 = ((s8[17694720]{0:T(1024)(128)(4,1)}), s8[4194304]{0:T(1024)(128)(4,1)S(1)}, s32[]{:S(2)}) async-start(s8[17694720]{0:T(1024)(128)(4,1)} %bitcast.427), calls=%async_computation.11 | async-start | bytes 8388608
  410.0 35.2 %slice-start.8 = ((s8[17694720]{0:T(1024)(128)(4,1)}), s8[4194304]{0:T(1024)(128)(4,1)S(1)}, s32[]{:S(2)}) async-start(s8[17694720]{0:T(1024)(128)(4,1)} %bitcast.427), calls=%async_computation.12 | async-start | bytes 8388608
  410.0 35.2 %slice-start.9 = ((s8[17694720]{0:T(1024)(128)(4,1)}), s8[917504]{0:T(1024)(128)(4,1)S(1)}, s32[]{:S(2)}) async-start(s8[17694720]{0:T(1024)(128)(4,1)} %bitcast.427), calls=%async_computation.13 | async-start | bytes 1835008
  445.3 34.6 %copy-start.3 = (f32[12,20,12,12]{1,0,3,2:T(8,128)S(1)}, f32[12,20,12,12]{1,0,3,2:T(8,128)}, u32[]{:S(2)}) copy-start(f32[12,20,12,12]{1,0,3,2:T(8,128)} %copy-done.2) | copy-start | bytes 414724
  445.3 34.6 %copy-start.4 = (f32[12,20,12,12]{1,0,3,2:T(8,128)S(1)}, f32[12,20,12,12]{1,0,3,2:T(8,128)}, u32[]{:S(2)}) copy-start(f32[12,20,12,12]{1,0,3,2:T(8,128)} %fusion.27) | copy-start | bytes 414724
  479.9 17.1 %copy-start.5 = (f32[12,12,12,1,20]{4,3,2,1,0:T(1,128)S(1)}, f32[12,12,12,1,20]{4,3,2,1,0:T(1,128)}, u32[]{:S(2)}) copy-start(f32[12,12,12,1,20]{4,3,2,1,0:T(1,128)} %fusion.2) | copy-start | bytes 414724
  510.6 92.4 %all-to-all-start.3 = ((f32[16,1,5760]{2,1,0:T(1,128)}), f32[16,1,5760]{2,1,0:T(1,128)S(1)}, u32[]{:S(2)}, u32[]{:S(2)}) async-start(f32[16,1,5760]{2,1,0:T(1,128)} %reshape.750), calls=%async_computation.3 | async-start | bytes 737280 | tf_op jit(solution)/shard_map/all_to_all | solution.py:91
  (15 other events, 31.6 us)
where the time goes:
time: 633 us; the launch traced here: 626 us
  matrix products  276 us (44%)
  local copies, waits for them, and re-layouts  187 us (30%)
  other arithmetic  61.2 us (10%)
  blocking collectives  59.8 us (9%)
  starting transfers between devices  21.6 us (3%)
  waiting for transfers between devices  18.8 us (3%)
    dot_general x11, matrix products, mult(): return jnp.einsum(form, left, right, precision=precise)  233 us
    unnamed x96, local copies, waits for them, and re-layouts  101 us
    psum x1, blocking collectives, local(): point_total, bias_total = lax.psum((point_local, bias_local), 'gx')  59.8 us
    another operation x2, other arithmetic, local(): spec_grad = jnp.stack([grad_real, grad_imag], axis=3)  47.5 us
    slice x1, local copies, waits for them, and re-layouts, local(): weight_real = spec_weight[:, :, :, 0]  37.5 us
    dot_general x32, matrix products, contract(): jnp.tensordot(wave_table, operand, axes=((1,), (position,)), precision=pr...  34.3 us
    all_to_all x6, local copies, waits for them, and re-layouts, to_grid(): lax.all_to_all(spread, 'gx', split_axis=0, concat_axis=4, tiled=True)  26.8 us
    another operation x4, local copies, waits for them, and re-layouts, complex_apply(): return jnp.stack([new_real, new_imag], axis=2)  16.8 us
  transfers between devices with their start and end apart: 4, of which 2 were waited for; matrix products, arithmetic and copies ran while one was open for 21% of the time, Pallas kernels for 0%

commit v1 on v0

v1 whole, which is shorter than its diff:
```python
import functools
import math

import jax
import jax.numpy as jnp
import numpy as np
from jax import lax
from jax.experimental import pallas as pl
from jax.experimental.pallas import tpu as pltpu
from jax.sharding import PartitionSpec as P

C = 20
MX = 12
MY = 12
MZ = 24
MT = 8
NZ = 32
NT = 16
NY = 16
ZT = NZ * NT
MZT = MZ * MT
CY = C * NY
HALF = MY // 2
LANES = 256
BF = jnp.bfloat16
F32 = jnp.float32
NN = ((1,), (0,))
NT_DIMS = ((1,), (1,))


def column(ky):
    return (ky // HALF) * 128 + (ky % HALF) * C


def freqs(count):
    modes = np.arange(count)
    return np.where(modes < count // 2, modes, modes - count)


def angles(count, length):
    phase = np.mod(freqs(count)[:, None] * np.arange(length)[None, :], length)
    return 2.0 * np.pi / length * phase


def halves(table):
    table = np.asarray(table, np.float64)
    high = table.astype(jnp.bfloat16)
    low = (table - high.astype(np.float64)).astype(jnp.bfloat16)
    return np.stack([high, low])


def depth_time(full_x, owners, doubled):
    scale = float(full_x * NY * ZT) ** (-0.5)
    modes = np.arange(MZT)
    depth = freqs(MZ)[modes // MT]
    time = modes % MT
    cells = np.arange(ZT)
    phase = depth[:, None] * (cells // NT)[None, :] * NT + time[:, None] * (cells % NT)[None, :] * NZ
    angle = 2.0 * np.pi / ZT * np.mod(phase, ZT)
    factor = np.full((MZT, 1), scale)
    if doubled:
        factor = factor * np.where(time == 0, 1.0, 2.0)[:, None]
    real, imag = factor * np.cos(angle), -factor * np.sin(angle)

    def rows(first, second):
        both = np.stack([first, second]).reshape(2, owners, MZT // owners, ZT)
        return both.transpose(1, 0, 2, 3).reshape(2 * MZT, ZT)

    return halves(np.stack([rows(real, imag), rows(imag, -real)]))


def y_tables():
    angle = angles(MY, NY)
    out = np.zeros((2, C, NY, LANES))
    for ky in range(MY):
        for c in range(C):
            out[0, c, :, column(ky) + c] = np.cos(angle[ky])
            out[1, c, :, column(ky) + c] = np.sin(angle[ky])
    return halves(out.reshape(2, CY, LANES))


def x_tables(full_x, owned):
    angle = angles(MX, full_x)
    cos, sin = np.cos(angle), np.sin(angle)
    eye = np.eye(owned)
    to_real = np.stack([cos, sin])
    to_imag = np.stack([-sin, cos])

    def lift(pair):
        grown = np.einsum("tpkx,mn->xpmntk", pair, eye)
        return grown.reshape(full_x * 2 * owned, owned * 2 * MX)

    even = lift(np.stack([to_real, to_imag]))
    odd = lift(np.stack([-to_imag, to_real]))
    modes = even.T
    from_real = np.stack([cos, sin])
    from_imag = np.stack([-sin, cos])
    lower = lift(np.stack([from_real, from_imag]))
    lower_odd = lift(np.stack([-from_imag, from_real]))
    return halves(np.stack([even, odd])), halves(modes), halves(np.stack([lower, lower_odd]))


def small_tables():
    place = np.zeros((2, C, NY, LANES))
    for i in range(C):
        j = i % 16
        place[i // 16, i, :, (j // 8) * 128 + 120 + j % 8] = 1.0
    spot = np.zeros((2, 2 * MZT, C, NY))
    for o in range(C):
        spot[0, 2 * o, o] = 1.0
        spot[1, 2 * o + 1, o] = 1.0
    return (
        place.reshape(2, CY, LANES).astype(jnp.bfloat16),
        spot.reshape(2, 2 * MZT, CY).astype(jnp.bfloat16),
    )


def split(value):
    high = value.astype(BF)
    return high, (value - high.astype(F32)).astype(BF)


def product(left, right, dims):
    def one(a, b):
        return lax.dot_general(a, b, (dims, ((), ())), preferred_element_type=F32)

    return one(left[0], right[0]) + (one(left[0], right[1]) + one(left[1], right[0]))


def table(ref, *index):
    return ref[(0,) + index], ref[(1,) + index]


def to_rows(field, depth_ref, y_ref):
    out = None
    for k in range(2):
        lifted = product(table(depth_ref, k), field, NT_DIMS)
        term = product(split(lifted), table(y_ref, k), NN)
        out = term if out is None else out + term
    return out


def to_cells(rows, depth_ref, y_ref):
    out = None
    for k in range(2):
        spread = product(table(y_ref, k), rows, NT_DIMS)
        term = product(split(spread), table(depth_ref, k), NN)
        out = term if out is None else out + term
    return out


def lift_kernel(field_ref, depth_ref, y_ref, out_ref):
    out_ref[...] = to_rows(split(field_ref[...]), depth_ref, y_ref)


def middle_kernel(
    rows_ref, field_ref, cot_ref, mix_ref, bias_ref, depth_ref, y_ref, place_ref, spot_ref,
    out_ref, dpre_ref, send_ref,
):
    field = split(field_ref[...])
    pre = to_cells(split(rows_ref[...]), depth_ref, y_ref)
    pre = pre + product(split(mix_ref[...]), field, NN) + bias_ref[...]
    cumulative = 0.5 * (1.0 + lax.erf(pre * (1.0 / math.sqrt(2.0))))
    density = jnp.exp(-0.5 * pre * pre) * (1.0 / math.sqrt(2.0 * math.pi))
    out_ref[...] = pre * cumulative
    dpre = cot_ref[...] * (cumulative + pre * density)
    dpre_ref[...] = dpre
    parts = split(dpre)
    send = to_rows(parts, depth_ref, y_ref)
    cross = product(parts, field, NT_DIMS)
    row = lax.broadcasted_iota(jnp.int32, (CY, CY), 0)
    col = lax.broadcasted_iota(jnp.int32, (CY, CY), 1)
    cross = split(jnp.where((row % NY) == (col % NY), cross, 0.0))
    lane = lax.broadcasted_iota(jnp.int32, (CY, LANES), 1)
    total = jnp.sum(dpre, axis=1, keepdims=True)
    for k in range(2):
        moved = jnp.dot(cross[0], place_ref[k], preferred_element_type=F32)
        moved = moved + jnp.dot(cross[1], place_ref[k], preferred_element_type=F32)
        if k == 1:
            moved = moved + jnp.where(lane == 124, total, 0.0)
        high, low = split(moved)
        send = send + jnp.dot(spot_ref[k], high, preferred_element_type=F32)
        send = send + jnp.dot(spot_ref[k], low, preferred_element_type=F32)
    send_ref[...] = send


def last_kernel(rows_ref, dpre_ref, mix_ref, depth_ref, y_ref, out_ref):
    grad = to_cells(split(rows_ref[...]), depth_ref, y_ref)
    out_ref[...] = grad + product(split(mix_ref[...]), split(dpre_ref[...]), NN)


def gather_kernel(owned, rows_ref, x_ref, ab_ref, even_ref, odd_ref):
    turned = split(rows_ref[...].T)
    even_ref[...] = product(turned, table(x_ref, 0), NN)
    odd_ref[...] = product(turned, table(x_ref, 1), NN)
    for m in range(owned):
        for p, ref in enumerate((even_ref, odd_ref)):
            part = ref[:, m * 24:(m + 1) * 24]
            part = jnp.concatenate([part, jnp.zeros((LANES, 104), F32)], axis=1)
            for ky in range(MY):
                ab_ref[m, pl.ds(ky * 40 + p, C, stride=2), :] = part[column(ky):column(ky) + C]


def mix_kernel(weight_ref, ab_ref, out_ref):
    def body(ky, carry):
        ab = ab_ref[0, pl.ds(pl.multiple_of(ky * 40, 8), 40), :]
        for kx in range(MX):
            start = pl.multiple_of(ky * 480 + kx * 40, 8)
            weight = weight_ref[pl.ds(start, 40), :]
            for p in range(2):
                lane = p * MX + kx
                out = jnp.sum(weight * ab[:, lane:lane + 1], axis=0, keepdims=True)
                out_ref[0, ky, lane:lane + 1, :] = out
        return carry

    lax.fori_loop(0, MY, body, 0)


def spread_kernel(owned, modes_ref, x_ref, out_ref, full_ref):
    full_ref[...] = jnp.zeros_like(full_ref)
    for ky in range(MY):
        part = modes_ref[:, ky].reshape(owned * 24, C)
        full_ref[:, column(ky):column(ky) + C] = part
    out_ref[...] = product(table(x_ref, 0), split(full_ref[...]), NN)


def back_modes_kernel(owned, rows_ref, x_ref, out_ref):
    modes = product(table(x_ref), split(rows_ref[...]), NN)
    for ky in range(MY):
        part = modes[:, column(ky):column(ky) + C]
        out_ref[:, ky] = part.reshape(owned, 24, C)


def grad_kernel(weight_ref, ab_ref, back_ref, grad_ref, sums_ref):
    lanes = lax.broadcasted_iota(jnp.int32, (40, 128), 1)

    def body(ky, carry):
        rows = pl.ds(pl.multiple_of(ky * 40, 8), 40)
        ab = ab_ref[0, rows, :]
        back = back_ref[0, ky]
        sums = jnp.zeros((40, 128), F32)
        for kx in range(MX):
            start = pl.multiple_of(ky * 480 + kx * 40, 8)
            weight = weight_ref[pl.ds(start, 40), :]
            real = back[kx:kx + 1, :]
            imag = back[MX + kx:MX + kx + 1, :]
            grad_ref[pl.ds(start, 40), :] = (
                ab[:, kx:kx + 1] * real + ab[:, MX + kx:MX + kx + 1] * imag
            )
            first = jnp.sum(weight * real, axis=1, keepdims=True)
            second = jnp.sum(weight * imag, axis=1, keepdims=True)
            sums = jnp.where(lanes == kx, first, sums)
            sums = jnp.where(lanes == MX + kx, second, sums)
        sums_ref[0, rows, :] = sums
        return carry

    lax.fori_loop(0, MY, body, 0)


def back_spread_kernel(owned, sums_ref, x_ref, rows_ref, out_ref, even_ref, odd_ref):
    even_ref[...] = jnp.zeros_like(even_ref)
    odd_ref[...] = jnp.zeros_like(odd_ref)
    for m in range(owned):
        for p, ref in enumerate((even_ref, odd_ref)):
            for ky in range(MY):
                part = sums_ref[m, pl.ds(ky * 40 + p, C, stride=2), :]
                ref[column(ky):column(ky) + C, m * 24:(m + 1) * 24] = part[:, :24]
    out = product(table(x_ref, 0), split(even_ref[...]), NT_DIMS)
    out = out + product(table(x_ref, 1), split(odd_ref[...]), NT_DIMS)
    peers, each, _ = rows_ref.shape
    lane = lax.broadcasted_iota(jnp.int32, (each, LANES), 1)
    total = jnp.where(lane % 128 >= 120, jnp.sum(rows_ref[...], axis=0), 0.0)
    for k in range(peers):
        out_ref[k] = out[k * each:(k + 1) * each] + total


PARAMS = pltpu.CompilerParams(vmem_limit_bytes=48 * 1024 * 1024)


def shaped(*shape):
    return jax.ShapeDtypeStruct(shape, F32)


def call(kernel, out_shape, name, scratch=()):
    return pl.pallas_call(
        kernel, out_shape=out_shape, scratch_shapes=list(scratch), compiler_params=PARAMS, name=name
    )


def local(state_field, cotangent, spec_weight, point_weight, bias_vector):
    peers = lax.axis_size("gx")
    owned = spec_weight.shape[0]
    full_x = state_field.shape[0] * peers
    norm_scale = float(full_x * NY * ZT) ** (-0.5)
    plain = depth_time(full_x, peers, False)
    double = depth_time(full_x, peers, True)
    y_table = y_tables()
    x_lift, x_modes, x_lower = x_tables(full_x, owned)
    place, spot = small_tables()

    rows_all = 2 * MZT
    width = owned * 24
    block = MY * MX * 2 * C
    field = state_field.reshape(CY, ZT)
    cot = cotangent.reshape(CY, ZT)
    weight = spec_weight.transpose(0, 1, 2, 4, 3, 5).reshape(owned * block, C)
    eye = jnp.eye(NY, dtype=F32)
    mix_in = jnp.einsum("oi,yz->iyoz", point_weight, eye, precision=lax.Precision.HIGHEST).reshape(CY, CY)
    mix_out = jnp.einsum("io,yz->iyoz", point_weight, eye, precision=lax.Precision.HIGHEST).reshape(CY, CY)
    bias = jnp.repeat(bias_vector, NY).reshape(CY, 1)

    def exchange(rows):
        cut = rows.reshape(peers, 2 * owned, LANES)
        return lax.all_to_all(cut, "gx", split_axis=0, concat_axis=0, tiled=True)

    weight_spec = pl.BlockSpec((block, C), lambda m: (m, 0))
    ab_spec = pl.BlockSpec((1, MY * 40, 128), lambda m: (m, 0, 0))
    modes_spec = pl.BlockSpec((1, MY, 24, C), lambda m: (m, 0, 0, 0))
    scratch = [pltpu.VMEM((LANES, width), F32)] * 2

    sent = call(lift_kernel, shaped(rows_all, LANES), "lift")(field, plain, y_table)
    got = exchange(sent).reshape(rows_all, LANES)
    ab = call(functools.partial(gather_kernel, owned), shaped(owned, MY * 40, 128), "x_modes", scratch)(got, x_lift)
    mixed = pl.pallas_call(
        mix_kernel, grid=(owned,), in_specs=[weight_spec, ab_spec], out_specs=modes_spec,
        out_shape=shaped(owned, MY, 24, C), compiler_params=PARAMS, name="mix",
    )(weight, ab)
    sent = call(
        functools.partial(spread_kernel, owned), shaped(rows_all, LANES), "x_rows",
        [pltpu.VMEM((width, LANES), F32)],
    )(mixed, x_lower)
    got = exchange(sent).reshape(rows_all, LANES)
    layer_out, dpre, sent = call(
        middle_kernel, (shaped(CY, ZT), shaped(CY, ZT), shaped(rows_all, LANES)), "middle"
    )(got, field, cot, mix_in, bias, double, y_table, place, spot)
    got = exchange(sent)
    back = call(
        functools.partial(back_modes_kernel, owned), shaped(owned, MY, 24, C), "back_modes"
    )(got.reshape(rows_all, LANES), x_modes)
    grad, sums = pl.pallas_call(
        grad_kernel, grid=(owned,), in_specs=[weight_spec, ab_spec, modes_spec],
        out_specs=(weight_spec, ab_spec),
        out_shape=(shaped(owned * block, C), shaped(owned, MY * 40, 128)),
        compiler_params=PARAMS, name="grads",
    )(weight, ab, back)
    sent = call(
        functools.partial(back_spread_kernel, owned), shaped(peers, 2 * owned, LANES), "back_rows", scratch
    )(sums, x_lower, got)
    got = exchange(sent).reshape(rows_all, LANES)
    field_grad = call(last_kernel, shaped(CY, ZT), "last")(got, dpre, mix_out, plain, y_table)
    small = got[:2 * C].reshape(C, 2, 2, 128)[..., 120:].reshape(C, 32) * norm_scale
    spec_grad = grad.reshape(owned, MY, MX, C, 2, C).transpose(0, 1, 2, 4, 3, 5)
    return (
        layer_out.reshape(state_field.shape),
        field_grad.reshape(state_field.shape),
        spec_grad,
        small[:, :C].T,
        small[:, C],
    )


def solution(mesh):
    in_specs = (
        P(("grp", "gx"), None, None, None),
        P(("grp", "gx"), None, None, None),
        P("gx", None, None, None, None, None),
        P(),
        P(),
    )
    out_specs = (
        P(("grp", "gx"), None, None, None),
        P(("grp", "gx"), None, None, None),
        P(("grp", "gx"), None, None, None, None, None),
        P("grp", None),
        P("grp"),
    )
    return jax.shard_map(local, mesh=mesh, in_specs=in_specs, out_specs=out_specs, check_vma=False)
```

time: 633 us -> 248 us (0.39)
  matrix products: 276 us -> 0 us
  Pallas kernels: 0 us -> 171 us
  local copies, waits for them, and re-layouts: 187 us -> 18.5 us
  other arithmetic: 61.2 us -> 2.45 us
  blocking collectives: 59.8 us -> 35.2 us
  starting transfers between devices: 21.6 us -> 7.24 us
  waiting for transfers between devices: 18.8 us -> 11.5 us
    dot_general x47 -> x0, matrix products: 276 us -> none  [the longest x11 233 us: mult(): return jnp.einsum(form, left, right, precision=precise)]
    pallas_call x0 -> x9, Pallas kernels: none -> 171 us  [the longest x1 112 us: local(): pl.pallas_call(grad_kernel, grid=(owned,), in_specs=[weight_spec, ab_spec...]
    unnamed x96 -> x35, local copies, waits for them, and re-layouts: 101 us -> 6.94 us
    psum x1 -> x0, blocking collectives: 59.8 us -> none  [local(): point_total, bias_total = lax.psum((point_local, bias_local), 'gx')]
    another operation x7 -> x1, other arithmetic: 48.8 us -> 0.01 us  [the longest x2 47.5 us: local(): spec_grad = jnp.stack([grad_real, grad_imag], axis=3)]
    slice x1 -> x2, local copies, waits for them, and re-layouts: 37.5 us -> 0.1 us  [local(): got[:2 * C].reshape(C, 2, 2, 128)[..., 120:].reshape(C, 32) * norm_scale]
    all_to_all x0 -> x2, blocking collectives: none -> 35.2 us  [exchange(): return lax.all_to_all(cut, 'gx', split_axis=0, concat_axis=0, tiled=True)]
    all_to_all x9 -> x0, local copies, waits for them, and re-layouts: 31.8 us -> none  [the longest x6 26.8 us: to_grid(): lax.all_to_all(spread, 'gx', split_axis=0, concat_axis=4, tiled=True)]
  transfers between devices with their start and end apart: 4 -> 2, of which waited for: 2 -> 2; matrix products, arithmetic and copies ran while one was open for 21% -> 5% of each run, Pallas kernels for 0% -> 0%
where the time goes in v1:
time: 248 us; the launch traced here: 247 us
  Pallas kernels  171 us (69%)
  blocking collectives  35.2 us (14%)
  local copies, waits for them, and re-layouts  18.5 us (7%)
  waiting for transfers between devices  11.5 us (5%)
  starting transfers between devices  7.24 us (3%)
    pallas_call x1, Pallas kernels, local(): pl.pallas_call(grad_kernel, grid=(owned,), in_specs=[weight_spec, ab_spec...  112 us
    pallas_call x1, Pallas kernels, local(): pl.pallas_call(mix_kernel, grid=(owned,), in_specs=[weight_spec, ab_spec]...  38.8 us
    all_to_all x2, blocking collectives, exchange(): return lax.all_to_all(cut, 'gx', split_axis=0, concat_axis=0, tiled=True)  35.2 us
    all_to_all x2, waiting for transfers between devices, exchange(): return lax.all_to_all(cut, 'gx', split_axis=0, concat_axis=0, tiled=True)  11.5 us
    pallas_call x1, Pallas kernels, local(): call(middle_kernel, (shaped(CY, ZT), shaped(CY, ZT), shaped(rows_all, LAN...  8.66 us
    all_to_all x2, starting transfers between devices, exchange(): return lax.all_to_all(cut, 'gx', split_axis=0, concat_axis=0, tiled=True)  7.24 us
    unnamed x35, local copies, waits for them, and re-layouts  6.94 us
  transfers between devices with their start and end apart: 2, of which 2 were waited for; matrix products, arithmetic and copies ran while one was open for 5% of the time, Pallas kernels for 0%

profile of v1, /device:TPU:0, one launch (start us, length us, event | category | flops | bytes accessed | tf_op | source)
XLA Modules:
  0.0 247.1 jit_solution(7537500053548331102)
XLA Ops:
  0.6 0.0 copy-start.1
  0.7 1.5 copy-done.3
  2.2 1.1 copy-done.5
  3.2 1.1 copy-done.7
  4.3 2.5 %lift.1 = f32[384,256]{1,0:T(8,128)S(1)} custom-call(f32[320,512]{1,0:T(8,128)S(1)} %bitcast.27, bf16[2,2,384,512]{3,2,1,0:T(8,128)(2,1)S(1)} %copy-done.3, bf16[2,2,320,256]{3,2,1,0:T(8,128)(2,1)S(1)} %copy-done.5), custom_call_target="tpu_custom_call" | custom-call | tf_op jit(solution)/shard_map/lift/pallas_call | solution.py:321
  6.9 19.4 %all_to_all.20 = f32[16,24,256]{2,1,0:T(8,128)S(1)} all-to-all(f32[16,24,256]{2,1,0:T(8,128)S(1)} %bitcast.32), channel_id=1, replica_groups=mesh['grp'=2,'gx'=16] {'gx'}, dimensions={0} | all-to-all | bytes 786432 | tf_op jit(solution)/shard_map/all_to_all | solution.py:314
  26.2 1.5 x_modes.1.ab_ref
  27.8 38.8 %mix.1.modes_ref = f32[12,12,24,20]{3,2,1,0:T(8,128)S(1)} custom-call(f32[69120,20]{1,0:T(8,128)} %bitcast.36, f32[12,480,128]{2,1,0:T(8,128)S(1)} %x_modes.1.ab_ref), custom_call_target="tpu_custom_call" | custom-call | tf_op jit(solution)/shard_map/mix/pallas_call | solution.py:324
  66.7 1.7 x_rows.1
  68.3 3.6 %all-to-all-start.1 = ((f32[16,24,256]{2,1,0:T(8,128)}), f32[16,24,256]{2,1,0:T(8,128)S(1)}, u32[]{:S(2)}, u32[]{:S(2)}) async-start(f32[16,24,256]{2,1,0:T(8,128)} %bitcast.5), calls=%async_computation.1 | async-start | bytes 786432 | tf_op jit(solution)/shard_map/all_to_all | solution.py:314
  71.9 0.1 broadcast_in_dim.3
  72.0 0.1 reshape_reshape.4.bias_ref
  72.1 2.4 multiply_bitcast_fusion
  74.6 3.9 %copy.23 = f32[20,16,20,16]{3,2,1,0:T(8,128)} copy(f32[20,16,20,16]{3,0,1,2:T(8,128)S(1)} %get-tuple-element.16) | data formatting | bytes 819200 | tf_op jit(solution)/shard_map/oi,yz->iyoz/transpose | solution.py:308
  78.4 3.2 %reshape.68.mix_ref = f32[320,320]{1,0:T(8,128)S(1)} reshape(f32[20,16,20,16]{3,2,1,0:T(8,128)} %copy.23) | data formatting | bytes 819200 | tf_op jit(solution)/shard_map/reshape | solution.py:308
  81.6 2.4 all-to-all-done.1
  84.1 1.1 copy-done.12
  85.1 1.0 copy-done.14
  86.1 8.7 %middle.1 = (f32[320,512]{1,0:T(8,128)}, f32[320,512]{1,0:T(8,128)S(1)}, f32[384,256]{1,0:T(8,128)S(1)}) custom-call(f32[384,256]{1,0:T(8,128)S(1)} %bitcast.33, f32[320,512]{1,0:T(8,128)S(1)} %bitcast.28, f32[320,512]{1,0:T(8,128)S(1)} %bitcast.34, f32[320,320]{1,0:T(8,128)S(1)} %reshape.68.mix_ref, f32[320,1]{1,0:T(8,128)S(1)} %reshape_reshape.4.bias_ref, ...), custom_call_target="tpu_custom_call" | custom-call | tf_op jit(solution)/shard_map/middle/pallas_call | solution.py:333
  94.8 15.8 %all_to_all.21.rows_ref = f32[16,24,256]{2,1,0:T(8,128)S(1)} all-to-all(f32[16,24,256]{2,1,0:T(8,128)S(1)} %bitcast.35), channel_id=1, replica_groups=mesh['grp'=2,'gx'=16] {'gx'}, dimensions={0} | all-to-all | bytes 786432 | tf_op jit(solution)/shard_map/all_to_all | solution.py:314
  110.6 0.8 back_modes.1.back_ref
  111.4 111.8 %grads.1 = (f32[69120,20]{1,0:T(8,128)}, f32[12,480,128]{2,1,0:T(8,128)S(1)}) custom-call(f32[69120,20]{1,0:T(8,128)} %bitcast.37, f32[12,480,128]{2,1,0:T(8,128)} %copy-done, f32[12,12,24,20]{3,2,1,0:T(8,128)S(1)} %back_modes.1.back_ref), custom_call_target="tpu_custom_call" | custom-call | tf_op jit(solution)/shard_map/grads/pallas_call | solution.py:340
  223.2 2.4 back_rows.1
  225.6 3.7 %all-to-all-start.3 = ((f32[16,24,256]{2,1,0:T(8,128)}), f32[16,24,256]{2,1,0:T(8,128)S(1)}, u32[]{:S(2)}, u32[]{:S(2)}) async-start(f32[16,24,256]{2,1,0:T(8,128)} %back_rows.1), calls=%async_computation.3 | async-start | bytes 786432 | tf_op jit(solution)/shard_map/all_to_all | solution.py:314
  229.3 3.1 %reshape.73.mix_ref = f32[320,320]{1,0:T(8,128)S(1)} reshape(f32[20,16,20,16]{3,2,1,0:T(8,128)} %get-tuple-element.15) | data formatting | bytes 819200 | tf_op jit(solution)/shard_map/reshape | solution.py:309
  232.3 9.1 %all-to-all-done.3 = f32[16,24,256]{2,1,0:T(8,128)S(1)} async-done(((f32[16,24,256]{2,1,0:T(8,128)}), f32[16,24,256]{2,1,0:T(8,128)S(1)}, u32[]{:S(2)}, u32[]{:S(2)}) %all-to-all-start.3) | async-done | bytes 393248 | tf_op jit(solution)/shard_map/all_to_all | solution.py:314
  241.5 0.1 slice.17
  241.6 0.1 copy.26
  241.7 0.5 slice_bitcast_fusion.1
  242.2 0.6 slice_bitcast_fusion
  242.8 1.1 copy-done.11
  243.9 3.2 %last.1 = f32[320,512]{1,0:T(8,128)} custom-call(f32[384,256]{1,0:T(8,128)S(1)} %bitcast.30, f32[320,512]{1,0:T(8,128)S(1)} %copy-done.11, f32[320,320]{1,0:T(8,128)S(1)} %reshape.73.mix_ref, bf16[2,2,384,512]{3,2,1,0:T(8,128)(2,1)S(1)} %copy-done.4, bf16[2,2,320,256]{3,2,1,0:T(8,128)(2,1)S(1)} %copy-done.6), custom_call_target="tpu_custom_call" | custom-call | tf_op jit(solution)/shard_map/last/pallas_call | solution.py:350
  (31 shorter events, 0.1 us)
Async XLA Ops:
  0.6 25.6 %copy-start.1 = (bf16[2,2,384,288]{3,2,1,0:T(8,128)(2,1)S(1)}, bf16[2,2,384,288]{3,2,1,0:T(8,128)(2,1)}, u32[]{:S(2)}) copy-start(bf16[2,2,384,288]{3,2,1,0:T(8,128)(2,1)} %constant.18.clone.x_ref) | copy-start | bytes 2654212
  0.6 1.5 copy-start.3
  2.1 1.1 copy-start.5
  3.2 1.1 copy-start.7
  27.8 38.8 %copy-start = (f32[12,480,128]{2,1,0:T(8,128)}, f32[12,480,128]{2,1,0:T(8,128)S(1)}, u32[]{:S(2)}) copy-start(f32[12,480,128]{2,1,0:T(8,128)S(1)} %x_modes.1.ab_ref) | copy-start | bytes 8847364
  66.6 5.3 %copy-start.16 = (f32[20]{0:T(128)S(1)}, f32[20]{0:T(128)}, u32[]{:S(2)}) copy-start(f32[20]{0:T(128)} %param.17) | copy-start | bytes 244
  66.6 5.5 %copy-start.15 = (f32[20,20]{1,0:T(8,128)S(1)}, f32[20,20]{1,0:T(8,128)}, u32[]{:S(2)}) copy-start(f32[20,20]{1,0:T(8,128)} %param.16) | copy-start | bytes 4804
  68.3 15.7 %all-to-all-start.1 = ((f32[16,24,256]{2,1,0:T(8,128)}), f32[16,24,256]{2,1,0:T(8,128)S(1)}, u32[]{:S(2)}, u32[]{:S(2)}) async-start(f32[16,24,256]{2,1,0:T(8,128)} %bitcast.5), calls=%async_computation.1 | async-start | bytes 786432 | tf_op jit(solution)/shard_map/all_to_all | solution.py:314
  78.4 5.6 %copy-start.6 = (bf16[2,2,320,256]{3,2,1,0:T(8,128)(2,1)S(1)}, bf16[2,2,320,256]{3,2,1,0:T(8,128)(2,1)}, u32[]{:S(2)}) copy-start(bf16[2,2,320,256]{3,2,1,0:T(8,128)(2,1)} %constant.17.clone.y_ref) | copy-start | bytes 1966084
  78.4 5.6 %copy-start.8 = (f32[1,20,16,512]{3,2,1,0:T(8,128)S(1)}, f32[1,20,16,512]{3,2,1,0:T(8,128)}, u32[]{:S(2)}) copy-start(f32[1,20,16,512]{3,2,1,0:T(8,128)} %param.13) | copy-start | bytes 1966084
  78.4 5.6 %copy-start.9 = (f32[1,20,16,512]{3,2,1,0:T(8,128)S(1)}, f32[1,20,16,512]{3,2,1,0:T(8,128)}, u32[]{:S(2)}) copy-start(f32[1,20,16,512]{3,2,1,0:T(8,128)} %param.14) | copy-start | bytes 1966084
  78.4 32.1 %copy-start.13 = (bf16[2,288,384]{2,1,0:T(8,128)(2,1)S(1)}, bf16[2,288,384]{2,1,0:T(8,128)(2,1)}, u32[]{:S(2)}) copy-start(bf16[2,288,384]{2,1,0:T(8,128)(2,1)} %constant.22.clone.x_ref) | copy-start | bytes 1327108
  84.1 1.1 copy-start.12
  85.1 1.0 copy-start.14
  94.8 128.4 %copy-start.10 = (f32[320,512]{1,0:T(8,128)}, f32[320,512]{1,0:T(8,128)S(1)}, u32[]{:S(2)}) copy-start(f32[320,512]{1,0:T(8,128)S(1)} %get-tuple-element.13.dpre_ref) | copy-start | bytes 1966084
  111.3 111.8 %copy-start.2 = (bf16[2,2,384,288]{3,2,1,0:T(8,128)(2,1)S(1)}, bf16[2,2,384,288]{3,2,1,0:T(8,128)(2,1)}, u32[]{:S(2)}) copy-start(bf16[2,2,384,288]{3,2,1,0:T(8,128)(2,1)} %constant.18.clone.x_ref) | copy-start | bytes 2654212
  225.6 17.2 %copy-start.4 = (bf16[2,2,384,512]{3,2,1,0:T(8,128)(2,1)S(1)}, bf16[2,2,384,512]{3,2,1,0:T(8,128)(2,1)}, u32[]{:S(2)}) copy-start(bf16[2,2,384,512]{3,2,1,0:T(8,128)(2,1)} %constant.16.clone.depth_ref) | copy-start | bytes 4718596
  225.6 15.9 %all-to-all-start.3 = ((f32[16,24,256]{2,1,0:T(8,128)}), f32[16,24,256]{2,1,0:T(8,128)S(1)}, u32[]{:S(2)}, u32[]{:S(2)}) async-start(f32[16,24,256]{2,1,0:T(8,128)} %back_rows.1), calls=%async_computation.3 | async-start | bytes 786432 | tf_op jit(solution)/shard_map/all_to_all | solution.py:314
  242.8 1.1 copy-start.11

commit v2 on v1

--- a/solution.py
+++ b/solution.py
@@ -196,24 +196,35 @@
     for m in range(owned):
         for p, ref in enumerate((even_ref, odd_ref)):
             part = ref[:, m * 24:(m + 1) * 24]
-            part = jnp.concatenate([part, jnp.zeros((LANES, 104), F32)], axis=1)
+            part = jnp.concatenate([part, part, part, jnp.zeros((LANES, 56), F32)], axis=1)
             for ky in range(MY):
                 ab_ref[m, pl.ds(ky * 40 + p, C, stride=2), :] = part[column(ky):column(ky) + C]
 
 
-def mix_kernel(weight_ref, ab_ref, out_ref):
-    def body(ky, carry):
-        ab = ab_ref[0, pl.ds(pl.multiple_of(ky * 40, 8), 40), :]
-        for kx in range(MX):
-            start = pl.multiple_of(ky * 480 + kx * 40, 8)
-            weight = weight_ref[pl.ds(start, 40), :]
-            for p in range(2):
-                lane = p * MX + kx
-                out = jnp.sum(weight * ab[:, lane:lane + 1], axis=0, keepdims=True)
-                out_ref[0, ky, lane:lane + 1, :] = out
-        return carry
-
-    lax.fori_loop(0, MY, body, 0)
+def pieces(ab):
+    high = ab.astype(BF).astype(F32)
+    lane = lax.broadcasted_iota(jnp.int32, ab.shape, 1)
+    return jnp.where((lane >= 24) & (lane < 48), ab - high, high)
+
+
+def stacked(value, order):
+    high = value.astype(BF).astype(F32)
+    parts = {"h": high, "l": value - high}
+    return jnp.concatenate([parts[k] for k in order], axis=0)
+
+
+def mix_kernel(weight_ref, ab_ref, tile_ref, out_ref):
+    row = lax.broadcasted_iota(jnp.int32, (48, 480), 0)
+    lane = lax.broadcasted_iota(jnp.int32, (48, 480), 1)
+    own = (row % MX) == (lane // 40)
+    for ky in range(MY):
+        ab = pieces(ab_ref[0, ky * 40:(ky + 1) * 40, :]).T[:48].astype(BF)
+        wide = jnp.dot(ab, tile_ref[...], preferred_element_type=F32)
+        wide = jnp.where(own, wide, 0.0).astype(BF)
+        high, low = split(weight_ref[ky * 480:(ky + 1) * 480, :])
+        out = jnp.dot(wide, high, preferred_element_type=F32)
+        out = out + jnp.dot(wide, low, preferred_element_type=F32)
+        out_ref[0, ky] = out[:24] + out[24:]
 
 
 def spread_kernel(owned, modes_ref, x_ref, out_ref, full_ref):
@@ -232,29 +243,25 @@
 
 
 def grad_kernel(weight_ref, ab_ref, back_ref, grad_ref, sums_ref):
-    lanes = lax.broadcasted_iota(jnp.int32, (40, 128), 1)
-
-    def body(ky, carry):
-        rows = pl.ds(pl.multiple_of(ky * 40, 8), 40)
-        ab = ab_ref[0, rows, :]
+    lane = lax.broadcasted_iota(jnp.int32, (480, 128), 1)
+    row = lax.broadcasted_iota(jnp.int32, (480, 128), 0)
+    own = (lane % MX) == (row // 40)
+    own_sums = own[:, :48]
+    for ky in range(MY):
+        ab = pieces(ab_ref[0, ky * 40:(ky + 1) * 40, :])
+        wide = jnp.where(own, jnp.concatenate([ab] * MX, axis=0), 0.0).astype(BF)
         back = back_ref[0, ky]
-        sums = jnp.zeros((40, 128), F32)
-        for kx in range(MX):
-            start = pl.multiple_of(ky * 480 + kx * 40, 8)
-            weight = weight_ref[pl.ds(start, 40), :]
-            real = back[kx:kx + 1, :]
-            imag = back[MX + kx:MX + kx + 1, :]
-            grad_ref[pl.ds(start, 40), :] = (
-                ab[:, kx:kx + 1] * real + ab[:, MX + kx:MX + kx + 1] * imag
-            )
-            first = jnp.sum(weight * real, axis=1, keepdims=True)
-            second = jnp.sum(weight * imag, axis=1, keepdims=True)
-            sums = jnp.where(lanes == kx, first, sums)
-            sums = jnp.where(lanes == MX + kx, second, sums)
-        sums_ref[0, rows, :] = sums
-        return carry
-
-    lax.fori_loop(0, MY, body, 0)
+        deep = jnp.concatenate([stacked(back, "hhl"), jnp.zeros((56, C), F32)], axis=0).astype(BF)
+        grad_ref[ky * 480:(ky + 1) * 480, :] = jnp.dot(wide, deep, preferred_element_type=F32)
+        across = stacked(back, "hl").astype(BF)
+        high, low = split(weight_ref[ky * 480:(ky + 1) * 480, :])
+        sums = lax.dot_general(high, across, (NT_DIMS, ((), ())), preferred_element_type=F32)
+        sums = sums + lax.dot_general(low, across, (NT_DIMS, ((), ())), preferred_element_type=F32)
+        sums = jnp.where(own_sums, sums, 0.0)
+        total = sums[:40]
+        for kx in range(1, MX):
+            total = total + sums[kx * 40:(kx + 1) * 40]
+        sums_ref[0, ky * 40:(ky + 1) * 40, 0:48] = total
 
 
 def back_spread_kernel(owned, sums_ref, x_ref, rows_ref, out_ref, even_ref, odd_ref):
@@ -264,7 +271,8 @@
         for p, ref in enumerate((even_ref, odd_ref)):
             for ky in range(MY):
                 part = sums_ref[m, pl.ds(ky * 40 + p, C, stride=2), :]
-                ref[column(ky):column(ky) + C, m * 24:(m + 1) * 24] = part[:, :24]
+                part = part[:, :24] + part[:, 24:48]
+                ref[column(ky):column(ky) + C, m * 24:(m + 1) * 24] = part
     out = product(table(x_ref, 0), split(even_ref[...]), NT_DIMS)
     out = out + product(table(x_ref, 1), split(odd_ref[...]), NT_DIMS)
     peers, each, _ = rows_ref.shape
@@ -315,6 +323,8 @@
 
     weight_spec = pl.BlockSpec((block, C), lambda m: (m, 0))
     ab_spec = pl.BlockSpec((1, MY * 40, 128), lambda m: (m, 0, 0))
+    tiling = np.tile(np.eye(2 * C), (1, MX)).astype(jnp.bfloat16)
+    tile_spec = pl.BlockSpec((2 * C, 2 * C * MX), lambda m: (0, 0))
     modes_spec = pl.BlockSpec((1, MY, 24, C), lambda m: (m, 0, 0, 0))
     scratch = [pltpu.VMEM((LANES, width), F32)] * 2
 
@@ -322,9 +332,9 @@
     got = exchange(sent).reshape(rows_all, LANES)
     ab = call(functools.partial(gather_kernel, owned), shaped(owned, MY * 40, 128), "x_modes", scratch)(got, x_lift)
     mixed = pl.pallas_call(
-        mix_kernel, grid=(owned,), in_specs=[weight_spec, ab_spec], out_specs=modes_spec,
+        mix_kernel, grid=(owned,), in_specs=[weight_spec, ab_spec, tile_spec], out_specs=modes_spec,
         out_shape=shaped(owned, MY, 24, C), compiler_params=PARAMS, name="mix",
-    )(weight, ab)
+    )(weight, ab, tiling)
     sent = call(
         functools.partial(spread_kernel, owned), shaped(rows_all, LANES), "x_rows",
         [pltpu.VMEM((width, LANES), F32)],

time: 248 us -> 169 us (0.68)
  Pallas kernels: 171 us -> 92.4 us
    pallas_call x1, Pallas kernels: 112 us -> 33 us  [local(): pl.pallas_call(grad_kernel, grid=(owned,), in_specs=[weight_spec, ab_spec...]
    pallas_call x1, Pallas kernels: 38.8 us -> 27.4 us  [local(): pl.pallas_call(mix_kernel, grid=(owned,), in_specs=[weight_spec, ab_spec,...]
    pallas_call x1, Pallas kernels: 2.38 us -> 11.9 us  [local(): call(functools.partial(back_spread_kernel, owned), shaped(peers, 2 * owne...]
    unnamed x35 -> x37, local copies, waits for them, and re-layouts: 6.94 us -> 6.95 us
  transfers between devices with their start and end apart: 2 -> 2, of which waited for: 2 -> 2; matrix products, arithmetic and copies ran while one was open for 5% -> 8% of each run, Pallas kernels for 0% -> 0%
where the time goes in v2:
time: 169 us; the launch traced here: 168 us
  Pallas kernels  92.4 us (55%)
  blocking collectives  35 us (21%)
  local copies, waits for them, and re-layouts  18.5 us (11%)
  waiting for transfers between devices  11.3 us (7%)
  starting transfers between devices  7.42 us (4%)
  other arithmetic  2.44 us (1%)
    all_to_all x2, blocking collectives, exchange(): return lax.all_to_all(cut, 'gx', split_axis=0, concat_axis=0, tiled=True)  35 us
    pallas_call x1, Pallas kernels, local(): pl.pallas_call(grad_kernel, grid=(owned,), in_specs=[weight_spec, ab_spec...  33 us
    pallas_call x1, Pallas kernels, local(): pl.pallas_call(mix_kernel, grid=(owned,), in_specs=[weight_spec, ab_spec,...  27.4 us
    pallas_call x1, Pallas kernels, local(): call(functools.partial(back_spread_kernel, owned), shaped(peers, 2 * owne...  11.9 us
    all_to_all x2, waiting for transfers between devices, exchange(): return lax.all_to_all(cut, 'gx', split_axis=0, concat_axis=0, tiled=True)  11.3 us
    pallas_call x1, Pallas kernels, local(): call(middle_kernel, (shaped(CY, ZT), shaped(CY, ZT), shaped(rows_all, LAN...  8.66 us
    all_to_all x2, starting transfers between devices, exchange(): return lax.all_to_all(cut, 'gx', split_axis=0, concat_axis=0, tiled=True)  7.42 us
    unnamed x37, local copies, waits for them, and re-layouts  6.95 us
  transfers between devices with their start and end apart: 2, of which 2 were waited for; matrix products, arithmetic and copies ran while one was open for 8% of the time, Pallas kernels for 0%

profile of v2, /device:TPU:0, one launch (start us, length us, event | category | flops | bytes accessed | tf_op | source)
XLA Modules:
  0.0 167.9 jit_solution(13499568980024316718)
XLA Ops:
  0.6 0.0 copy-start.1
  0.7 1.5 copy-done.3
  2.2 1.1 copy-done.5
  3.2 1.1 copy-done.7
  4.3 2.5 %lift.1 = f32[384,256]{1,0:T(8,128)S(1)} custom-call(f32[320,512]{1,0:T(8,128)S(1)} %bitcast.27, bf16[2,2,384,512]{3,2,1,0:T(8,128)(2,1)S(1)} %copy-done.3, bf16[2,2,320,256]{3,2,1,0:T(8,128)(2,1)S(1)} %copy-done.5), custom_call_target="tpu_custom_call" | custom-call | tf_op jit(solution)/shard_map/lift/pallas_call | solution.py:331
  6.9 19.4 %all_to_all.20 = f32[16,24,256]{2,1,0:T(8,128)S(1)} all-to-all(f32[16,24,256]{2,1,0:T(8,128)S(1)} %bitcast.32), channel_id=1, replica_groups=mesh['grp'=2,'gx'=16] {'gx'}, dimensions={0} | all-to-all | bytes 786432 | tf_op jit(solution)/shard_map/all_to_all | solution.py:322
  26.3 3.2 %x_modes.1.ab_ref = f32[12,480,128]{2,1,0:T(8,128)S(1)} custom-call(f32[384,256]{1,0:T(8,128)S(1)} %bitcast.31, bf16[2,2,384,288]{3,2,1,0:T(8,128)(2,1)S(1)} %copy-done.1), custom_call_target="tpu_custom_call" | custom-call | tf_op jit(solution)/shard_map/x_modes/pallas_call | solution.py:333
  29.5 27.4 %mix.1.modes_ref = f32[12,12,24,20]{3,2,1,0:T(8,128)S(1)} custom-call(f32[69120,20]{1,0:T(8,128)} %bitcast.36, f32[12,480,128]{2,1,0:T(8,128)S(1)} %x_modes.1.ab_ref, bf16[40,480]{1,0:T(8,128)(2,1)S(1)} %copy-done.15), custom_call_target="tpu_custom_call" | custom-call | tf_op jit(solution)/shard_map/mix/pallas_call | solution.py:334
  56.9 1.7 %x_rows.1 = f32[384,256]{1,0:T(8,128)} custom-call(f32[12,12,24,20]{3,2,1,0:T(8,128)S(1)} %mix.1.modes_ref, bf16[2,2,384,288]{3,2,1,0:T(8,128)(2,1)S(1)} %copy-done.1), custom_call_target="tpu_custom_call" | custom-call | tf_op jit(solution)/shard_map/x_rows/pallas_call | solution.py:338
  58.6 3.7 %all-to-all-start.1 = ((f32[16,24,256]{2,1,0:T(8,128)}), f32[16,24,256]{2,1,0:T(8,128)S(1)}, u32[]{:S(2)}, u32[]{:S(2)}) async-start(f32[16,24,256]{2,1,0:T(8,128)} %bitcast.5), calls=%async_computation.1 | async-start | bytes 786432 | tf_op jit(solution)/shard_map/all_to_all | solution.py:322
  62.4 0.1 broadcast_in_dim.3
  62.4 0.1 reshape_reshape.4.bias_ref
  62.6 2.4 %multiply_bitcast_fusion = (f32[20,16,20,16]{3,2,1,0:T(8,128)}, f32[20,16,20,16]{3,0,1,2:T(8,128)S(1)}) fusion(f32[20,20]{1,0:T(8,128)S(1)} %copy-done.16, f32[16,16]{1,0:T(8,128)S(1)} %fusion), kind=kLoop, calls=%fused_computation | loop fusion | flops 102400 | bytes 821824 | tf_op jit(solution)/shard_map/io,yz->iyoz/transpose | solution.py:317
  65.0 3.9 %copy.24 = f32[20,16,20,16]{3,2,1,0:T(8,128)} copy(f32[20,16,20,16]{3,0,1,2:T(8,128)S(1)} %get-tuple-element.16) | data formatting | bytes 819200 | tf_op jit(solution)/shard_map/oi,yz->iyoz/transpose | solution.py:316
  68.9 3.2 %reshape.68.mix_ref = f32[320,320]{1,0:T(8,128)S(1)} reshape(f32[20,16,20,16]{3,2,1,0:T(8,128)} %copy.24) | data formatting | bytes 819200 | tf_op jit(solution)/shard_map/reshape | solution.py:316
  72.1 2.2 %all-to-all-done.1 = f32[16,24,256]{2,1,0:T(8,128)S(1)} async-done(((f32[16,24,256]{2,1,0:T(8,128)}), f32[16,24,256]{2,1,0:T(8,128)S(1)}, u32[]{:S(2)}, u32[]{:S(2)}) %all-to-all-start.1) | async-done | bytes 393248 | tf_op jit(solution)/shard_map/all_to_all | solution.py:322
  74.4 1.1 copy-done.12
  75.4 1.0 copy-done.14
  76.4 8.7 %middle.1 = (f32[320,512]{1,0:T(8,128)}, f32[320,512]{1,0:T(8,128)S(1)}, f32[384,256]{1,0:T(8,128)S(1)}) custom-call(f32[384,256]{1,0:T(8,128)S(1)} %bitcast.33, f32[320,512]{1,0:T(8,128)S(1)} %bitcast.28, f32[320,512]{1,0:T(8,128)S(1)} %bitcast.34, f32[320,320]{1,0:T(8,128)S(1)} %reshape.68.mix_ref, f32[320,1]{1,0:T(8,128)S(1)} %reshape_reshape.4.bias_ref, ...), custom_call_target="tpu_custom_call" | custom-call | tf_op jit(solution)/shard_map/middle/pallas_call | solution.py:343
  85.1 15.6 %all_to_all.21.rows_ref = f32[16,24,256]{2,1,0:T(8,128)S(1)} all-to-all(f32[16,24,256]{2,1,0:T(8,128)S(1)} %bitcast.35), channel_id=1, replica_groups=mesh['grp'=2,'gx'=16] {'gx'}, dimensions={0} | all-to-all | bytes 786432 | tf_op jit(solution)/shard_map/all_to_all | solution.py:322
  100.7 0.8 back_modes.1.back_ref
  101.5 33.0 %grads.1 = (f32[69120,20]{1,0:T(8,128)}, f32[12,480,128]{2,1,0:T(8,128)S(1)}) custom-call(f32[69120,20]{1,0:T(8,128)} %bitcast.37, f32[12,480,128]{2,1,0:T(8,128)} %copy-done, f32[12,12,24,20]{3,2,1,0:T(8,128)S(1)} %back_modes.1.back_ref), custom_call_target="tpu_custom_call" | custom-call | tf_op jit(solution)/shard_map/grads/pallas_call | solution.py:350
  134.5 11.9 %back_rows.1 = f32[16,24,256]{2,1,0:T(8,128)} custom-call(f32[12,480,128]{2,1,0:T(8,128)S(1)} %get-tuple-element.12.sums_ref, bf16[2,2,384,288]{3,2,1,0:T(8,128)(2,1)S(1)} %copy-done.2, f32[16,24,256]{2,1,0:T(8,128)S(1)} %all_to_all.21.rows_ref), custom_call_target="tpu_custom_call" | custom-call | tf_op jit(solution)/shard_map/back_rows/pallas_call | solution.py:356
  146.4 3.7 %all-to-all-start.3 = ((f32[16,24,256]{2,1,0:T(8,128)}), f32[16,24,256]{2,1,0:T(8,128)S(1)}, u32[]{:S(2)}, u32[]{:S(2)}) async-start(f32[16,24,256]{2,1,0:T(8,128)} %back_rows.1), calls=%async_computation.3 | async-start | bytes 786432 | tf_op jit(solution)/shard_map/all_to_all | solution.py:322
  150.1 3.1 %reshape.73.mix_ref = f32[320,320]{1,0:T(8,128)S(1)} reshape(f32[20,16,20,16]{3,2,1,0:T(8,128)} %get-tuple-element.15) | data formatting | bytes 819200 | tf_op jit(solution)/shard_map/reshape | solution.py:317
  153.1 9.1 %all-to-all-done.3 = f32[16,24,256]{2,1,0:T(8,128)S(1)} async-done(((f32[16,24,256]{2,1,0:T(8,128)}), f32[16,24,256]{2,1,0:T(8,128)S(1)}, u32[]{:S(2)}, u32[]{:S(2)}) %all-to-all-start.3) | async-done | bytes 393248 | tf_op jit(solution)/shard_map/all_to_all | solution.py:322
  162.3 0.1 slice.17
  162.4 0.1 copy.27
  162.5 0.5 slice_bitcast_fusion.1
  163.0 0.6 slice_bitcast_fusion
  163.6 1.1 copy-done.11
  164.7 3.2 %last.1 = f32[320,512]{1,0:T(8,128)} custom-call(f32[384,256]{1,0:T(8,128)S(1)} %bitcast.30, f32[320,512]{1,0:T(8,128)S(1)} %copy-done.11, f32[320,320]{1,0:T(8,128)S(1)} %reshape.73.mix_ref, bf16[2,2,384,512]{3,2,1,0:T(8,128)(2,1)S(1)} %copy-done.4, bf16[2,2,320,256]{3,2,1,0:T(8,128)(2,1)S(1)} %copy-done.6), custom_call_target="tpu_custom_call" | custom-call | tf_op jit(solution)/shard_map/last/pallas_call | solution.py:360
  (33 shorter events, 0.1 us)
Async XLA Ops:
  0.6 25.6 %copy-start.1 = (bf16[2,2,384,288]{3,2,1,0:T(8,128)(2,1)S(1)}, bf16[2,2,384,288]{3,2,1,0:T(8,128)(2,1)}, u32[]{:S(2)}) copy-start(bf16[2,2,384,288]{3,2,1,0:T(8,128)(2,1)} %constant.20.clone.x_ref) | copy-start | bytes 2654212
  0.6 1.5 copy-start.3
  2.1 1.1 copy-start.5
  3.2 1.1 copy-start.7
  4.3 25.1 %copy-start.15 = (bf16[40,480]{1,0:T(8,128)(2,1)S(1)}, bf16[40,480]{1,0:T(8,128)(2,1)}, u32[]{:S(2)}) copy-start(bf16[40,480]{1,0:T(8,128)(2,1)} %constant.21.clone.tile_ref) | copy-start | bytes 115204
  29.4 27.5 %copy-start = (f32[12,480,128]{2,1,0:T(8,128)}, f32[12,480,128]{2,1,0:T(8,128)S(1)}, u32[]{:S(2)}) copy-start(f32[12,480,128]{2,1,0:T(8,128)S(1)} %x_modes.1.ab_ref) | copy-start | bytes 8847364
  56.9 5.5 %copy-start.17 = (f32[20]{0:T(128)S(1)}, f32[20]{0:T(128)}, u32[]{:S(2)}) copy-start(f32[20]{0:T(128)} %param.18) | copy-start | bytes 244
  56.9 5.7 %copy-start.16 = (f32[20,20]{1,0:T(8,128)S(1)}, f32[20,20]{1,0:T(8,128)}, u32[]{:S(2)}) copy-start(f32[20,20]{1,0:T(8,128)} %param.17) | copy-start | bytes 4804
  58.6 15.7 %all-to-all-start.1 = ((f32[16,24,256]{2,1,0:T(8,128)}), f32[16,24,256]{2,1,0:T(8,128)S(1)}, u32[]{:S(2)}, u32[]{:S(2)}) async-start(f32[16,24,256]{2,1,0:T(8,128)} %bitcast.5), calls=%async_computation.1 | async-start | bytes 786432 | tf_op jit(solution)/shard_map/all_to_all | solution.py:322
  68.9 5.5 %copy-start.6 = (bf16[2,2,320,256]{3,2,1,0:T(8,128)(2,1)S(1)}, bf16[2,2,320,256]{3,2,1,0:T(8,128)(2,1)}, u32[]{:S(2)}) copy-start(bf16[2,2,320,256]{3,2,1,0:T(8,128)(2,1)} %constant.19.clone.y_ref) | copy-start | bytes 1966084
  68.9 5.5 %copy-start.8 = (f32[1,20,16,512]{3,2,1,0:T(8,128)S(1)}, f32[1,20,16,512]{3,2,1,0:T(8,128)}, u32[]{:S(2)}) copy-start(f32[1,20,16,512]{3,2,1,0:T(8,128)} %param.14) | copy-start | bytes 1966084
  68.9 5.5 %copy-start.9 = (f32[1,20,16,512]{3,2,1,0:T(8,128)S(1)}, f32[1,20,16,512]{3,2,1,0:T(8,128)}, u32[]{:S(2)}) copy-start(f32[1,20,16,512]{3,2,1,0:T(8,128)} %param.15) | copy-start | bytes 1966084
  68.9 31.8 %copy-start.13 = (bf16[2,288,384]{2,1,0:T(8,128)(2,1)S(1)}, bf16[2,288,384]{2,1,0:T(8,128)(2,1)}, u32[]{:S(2)}) copy-start(bf16[2,288,384]{2,1,0:T(8,128)(2,1)} %constant.25.clone.x_ref) | copy-start | bytes 1327108
  74.3 1.1 copy-start.12
  75.4 1.0 copy-start.14
  85.1 49.4 %copy-start.10 = (f32[320,512]{1,0:T(8,128)}, f32[320,512]{1,0:T(8,128)S(1)}, u32[]{:S(2)}) copy-start(f32[320,512]{1,0:T(8,128)S(1)} %get-tuple-element.13.dpre_ref) | copy-start | bytes 1966084
  101.4 33.0 %copy-start.2 = (bf16[2,2,384,288]{3,2,1,0:T(8,128)(2,1)S(1)}, bf16[2,2,384,288]{3,2,1,0:T(8,128)(2,1)}, u32[]{:S(2)}) copy-start(bf16[2,2,384,288]{3,2,1,0:T(8,128)(2,1)} %constant.20.clone.x_ref) | copy-start | bytes 2654212
  146.4 17.2 %copy-start.4 = (bf16[2,2,384,512]{3,2,1,0:T(8,128)(2,1)S(1)}, bf16[2,2,384,512]{3,2,1,0:T(8,128)(2,1)}, u32[]{:S(2)}) copy-start(bf16[2,2,384,512]{3,2,1,0:T(8,128)(2,1)} %constant.18.clone.depth_ref) | copy-start | bytes 4718596
  146.4 15.9 %all-to-all-start.3 = ((f32[16,24,256]{2,1,0:T(8,128)}), f32[16,24,256]{2,1,0:T(8,128)S(1)}, u32[]{:S(2)}, u32[]{:S(2)}) async-start(f32[16,24,256]{2,1,0:T(8,128)} %back_rows.1), calls=%async_computation.3 | async-start | bytes 786432 | tf_op jit(solution)/shard_map/all_to_all | solution.py:322
  163.6 1.1 copy-start.11

commit v3 on v2

--- a/solution.py
+++ b/solution.py
@@ -149,17 +149,67 @@
     return out
 
 
+def pointwise(weight_ref, repeat_ref, dims):
+    row = lax.broadcasted_iota(jnp.int32, (CY, CY), 0)
+    lane = lax.broadcasted_iota(jnp.int32, (CY, CY), 1)
+    repeat = repeat_ref[...]
+
+    def one(part):
+        tall = lax.dot_general(repeat, part, (dims, ((), ())), preferred_element_type=F32).astype(BF)
+        full = lax.dot_general(tall, repeat, (NT_DIMS, ((), ())), preferred_element_type=F32)
+        return jnp.where((row % NY) == (lane % NY), full, 0.0).astype(BF)
+
+    high, low = split(weight_ref[...])
+    return one(high), one(low)
+
+
+def exchange_kernel(rows_ref, out_ref, send_sem, recv_sem, own_sem):
+    peers = rows_ref.shape[0]
+    me = lax.axis_index("gx")
+    barrier = pltpu.get_barrier_semaphore()
+
+    def greet(k, carry):
+        pl.semaphore_signal(
+            barrier, inc=1, device_id={"gx": lax.rem(me + k, peers)},
+            device_id_type=pl.DeviceIdType.MESH,
+        )
+        return carry
+
+    def moved(k):
+        peer = lax.rem(me + k, peers)
+        return pltpu.make_async_remote_copy(
+            src_ref=rows_ref.at[peer], dst_ref=out_ref.at[me], send_sem=send_sem.at[k],
+            recv_sem=recv_sem.at[k], device_id={"gx": peer}, device_id_type=pl.DeviceIdType.MESH,
+        )
+
+    def begin(k, carry):
+        moved(k).start()
+        return carry
+
+    def finish(k, carry):
+        moved(k).wait()
+        return carry
+
+    lax.fori_loop(1, peers, greet, 0)
+    own = pltpu.make_async_copy(rows_ref.at[me], out_ref.at[me], own_sem)
+    own.start()
+    pl.semaphore_wait(barrier, peers - 1)
+    lax.fori_loop(1, peers, begin, 0)
+    own.wait()
+    lax.fori_loop(1, peers, finish, 0)
+
+
 def lift_kernel(field_ref, depth_ref, y_ref, out_ref):
     out_ref[...] = to_rows(split(field_ref[...]), depth_ref, y_ref)
 
 
 def middle_kernel(
-    rows_ref, field_ref, cot_ref, mix_ref, bias_ref, depth_ref, y_ref, place_ref, spot_ref,
+    rows_ref, field_ref, cot_ref, mix_ref, repeat_ref, bias_ref, depth_ref, y_ref, place_ref, spot_ref,
     out_ref, dpre_ref, send_ref,
 ):
     field = split(field_ref[...])
     pre = to_cells(split(rows_ref[...]), depth_ref, y_ref)
-    pre = pre + product(split(mix_ref[...]), field, NN) + bias_ref[...]
+    pre = pre + product(pointwise(mix_ref, repeat_ref, NT_DIMS), field, NN) + bias_ref[...]
     cumulative = 0.5 * (1.0 + lax.erf(pre * (1.0 / math.sqrt(2.0))))
     density = jnp.exp(-0.5 * pre * pre) * (1.0 / math.sqrt(2.0 * math.pi))
     out_ref[...] = pre * cumulative
@@ -184,9 +234,9 @@
     send_ref[...] = send
 
 
-def last_kernel(rows_ref, dpre_ref, mix_ref, depth_ref, y_ref, out_ref):
+def last_kernel(rows_ref, dpre_ref, mix_ref, repeat_ref, depth_ref, y_ref, out_ref):
     grad = to_cells(split(rows_ref[...]), depth_ref, y_ref)
-    out_ref[...] = grad + product(split(mix_ref[...]), split(dpre_ref[...]), NN)
+    out_ref[...] = grad + product(pointwise(mix_ref, repeat_ref, NN), split(dpre_ref[...]), NN)
 
 
 def gather_kernel(owned, rows_ref, x_ref, ab_ref, even_ref, odd_ref):
@@ -261,7 +311,7 @@
         total = sums[:40]
         for kx in range(1, MX):
             total = total + sums[kx * 40:(kx + 1) * 40]
-        sums_ref[0, ky * 40:(ky + 1) * 40, 0:48] = total
+        sums_ref[0, ky * 40:(ky + 1) * 40, 0:24] = total[:, :24] + total[:, 24:]
 
 
 def back_spread_kernel(owned, sums_ref, x_ref, rows_ref, out_ref, even_ref, odd_ref):
@@ -271,8 +321,7 @@
         for p, ref in enumerate((even_ref, odd_ref)):
             for ky in range(MY):
                 part = sums_ref[m, pl.ds(ky * 40 + p, C, stride=2), :]
-                part = part[:, :24] + part[:, 24:48]
-                ref[column(ky):column(ky) + C, m * 24:(m + 1) * 24] = part
+                ref[column(ky):column(ky) + C, m * 24:(m + 1) * 24] = part[:, :24]
     out = product(table(x_ref, 0), split(even_ref[...]), NT_DIMS)
     out = out + product(table(x_ref, 1), split(odd_ref[...]), NT_DIMS)
     peers, each, _ = rows_ref.shape
@@ -312,14 +361,23 @@
     field = state_field.reshape(CY, ZT)
     cot = cotangent.reshape(CY, ZT)
     weight = spec_weight.transpose(0, 1, 2, 4, 3, 5).reshape(owned * block, C)
-    eye = jnp.eye(NY, dtype=F32)
-    mix_in = jnp.einsum("oi,yz->iyoz", point_weight, eye, precision=lax.Precision.HIGHEST).reshape(CY, CY)
-    mix_out = jnp.einsum("io,yz->iyoz", point_weight, eye, precision=lax.Precision.HIGHEST).reshape(CY, CY)
+    repeat = np.repeat(np.eye(C), NY, axis=0).astype(jnp.bfloat16)
     bias = jnp.repeat(bias_vector, NY).reshape(CY, 1)
 
-    def exchange(rows):
+    def exchange(rows, collective_id):
         cut = rows.reshape(peers, 2 * owned, LANES)
-        return lax.all_to_all(cut, "gx", split_axis=0, concat_axis=0, tiled=True)
+        return pl.pallas_call(
+            exchange_kernel,
+            out_shape=jax.ShapeDtypeStruct(cut.shape, F32),
+            in_specs=[pl.BlockSpec(memory_space=pltpu.VMEM)],
+            out_specs=pl.BlockSpec(memory_space=pltpu.VMEM),
+            scratch_shapes=[
+                pltpu.SemaphoreType.DMA((peers,)), pltpu.SemaphoreType.DMA((peers,)),
+                pltpu.SemaphoreType.DMA,
+            ],
+            compiler_params=pltpu.CompilerParams(collective_id=collective_id, has_side_effects=True),
+            name="exchange",
+        )(cut)
 
     weight_spec = pl.BlockSpec((block, C), lambda m: (m, 0))
     ab_spec = pl.BlockSpec((1, MY * 40, 128), lambda m: (m, 0, 0))
@@ -329,7 +387,7 @@
     scratch = [pltpu.VMEM((LANES, width), F32)] * 2
 
     sent = call(lift_kernel, shaped(rows_all, LANES), "lift")(field, plain, y_table)
-    got = exchange(sent).reshape(rows_all, LANES)
+    got = exchange(sent, 0).reshape(rows_all, LANES)
     ab = call(functools.partial(gather_kernel, owned), shaped(owned, MY * 40, 128), "x_modes", scratch)(got, x_lift)
     mixed = pl.pallas_call(
         mix_kernel, grid=(owned,), in_specs=[weight_spec, ab_spec, tile_spec], out_specs=modes_spec,
@@ -339,11 +397,11 @@
         functools.partial(spread_kernel, owned), shaped(rows_all, LANES), "x_rows",
         [pltpu.VMEM((width, LANES), F32)],
     )(mixed, x_lower)
-    got = exchange(sent).reshape(rows_all, LANES)
+    got = exchange(sent, 1).reshape(rows_all, LANES)
     layer_out, dpre, sent = call(
         middle_kernel, (shaped(CY, ZT), shaped(CY, ZT), shaped(rows_all, LANES)), "middle"
-    )(got, field, cot, mix_in, bias, double, y_table, place, spot)
-    got = exchange(sent)
+    )(got, field, cot, point_weight, repeat, bias, double, y_table, place, spot)
+    got = exchange(sent, 2)
     back = call(
         functools.partial(back_modes_kernel, owned), shaped(owned, MY, 24, C), "back_modes"
     )(got.reshape(rows_all, LANES), x_modes)
@@ -356,8 +414,8 @@
     sent = call(
         functools.partial(back_spread_kernel, owned), shaped(peers, 2 * owned, LANES), "back_rows", scratch
     )(sums, x_lower, got)
-    got = exchange(sent).reshape(rows_all, LANES)
-    field_grad = call(last_kernel, shaped(CY, ZT), "last")(got, dpre, mix_out, plain, y_table)
+    got = exchange(sent, 3).reshape(rows_all, LANES)
+    field_grad = call(last_kernel, shaped(CY, ZT), "last")(got, dpre, point_weight, repeat, plain, y_table)
     small = got[:2 * C].reshape(C, 2, 2, 128)[..., 120:].reshape(C, 32) * norm_scale
     spec_grad = grad.reshape(owned, MY, MX, C, 2, C).transpose(0, 1, 2, 4, 3, 5)
     return (

time: 169 us -> 163 us (0.964)
  Pallas kernels: 92.4 us -> 141 us
  blocking collectives: 35 us -> 0 us
  waiting for transfers between devices: 11.3 us -> 0 us
  starting transfers between devices: 7.42 us -> 0 us
  other arithmetic: 2.44 us -> 0.01 us
    pallas_call x0 -> x4, Pallas kernels: none -> 60.1 us  [exchange(): pl.pallas_call(exchange_kernel, out_shape=jax.ShapeDtypeStruct(cut.shape,...]
    all_to_all x2 -> x0, blocking collectives: 35 us -> none  [exchange(): return lax.all_to_all(cut, 'gx', split_axis=0, concat_axis=0, tiled=True)]
    all_to_all x2 -> x0, waiting for transfers between devices: 11.3 us -> none  [exchange(): return lax.all_to_all(cut, 'gx', split_axis=0, concat_axis=0, tiled=True)]
    unnamed x37 -> x55, local copies, waits for them, and re-layouts: 6.95 us -> 17.7 us
    pallas_call x1, Pallas kernels: 11.9 us -> 1.63 us  [local(): call(functools.partial(back_spread_kernel, owned), shaped(peers, 2 * owne...]
    all_to_all x2 -> x0, starting transfers between devices: 7.42 us -> none  [exchange(): return lax.all_to_all(cut, 'gx', split_axis=0, concat_axis=0, tiled=True)]
    reshape x2 -> x0, local copies, waits for them, and re-layouts: 6.27 us -> none  [the longest x1 3.21 us: local(): jnp.einsum('oi,yz->iyoz', point_weight, eye, precision=lax.Precision.HIGH...]
    transpose x1 -> x0, local copies, waits for them, and re-layouts: 3.86 us -> none  [local(): jnp.einsum('oi,yz->iyoz', point_weight, eye, precision=lax.Precision.HIGH...]
  transfers between devices with their start and end apart: 2 -> 0, of which waited for: 2 -> 0; matrix products, arithmetic and copies ran while one was open for 8% -> 0% of each run, Pallas kernels for 0% -> 0%
where the time goes in v3:
time: 163 us; the launch traced here: 162 us
  Pallas kernels  141 us (87%)
  local copies, waits for them, and re-layouts  19.7 us (12%)
    pallas_call x4, Pallas kernels, exchange(): pl.pallas_call(exchange_kernel, out_shape=jax.ShapeDtypeStruct(cut.shape,...  60.1 us
    pallas_call x1, Pallas kernels, local(): pl.pallas_call(grad_kernel, grid=(owned,), in_specs=[weight_spec, ab_spec...  33.1 us
    pallas_call x1, Pallas kernels, local(): pl.pallas_call(mix_kernel, grid=(owned,), in_specs=[weight_spec, ab_spec,...  27.4 us
    unnamed x55, local copies, waits for them, and re-layouts  17.7 us
    pallas_call x1, Pallas kernels, local(): call(middle_kernel, (shaped(CY, ZT), shaped(CY, ZT), shaped(rows_all, LAN...  7.75 us
    pallas_call x1, Pallas kernels, local(): call(last_kernel, shaped(CY, ZT), 'last')  3.68 us

profile of v3, /device:TPU:0, one launch (start us, length us, event | category | flops | bytes accessed | tf_op | source)
XLA Modules:
  0.0 161.8 jit_solution(11058293706644806106)
XLA Ops:
  0.6 0.7 broadcast_in_dim.3
  1.5 1.4 copy-done.4
  2.9 1.1 copy-done.6
  4.0 1.1 copy-done.10
  5.1 2.5 %lift.1 = f32[384,256]{1,0:T(8,128)S(1)} custom-call(f32[320,512]{1,0:T(8,128)S(1)} %bitcast.23, bf16[2,2,384,512]{3,2,1,0:T(8,128)(2,1)S(1)} %copy-done.4, bf16[2,2,320,256]{3,2,1,0:T(8,128)(2,1)S(1)} %copy-done.6), custom_call_target="tpu_custom_call" | custom-call | tf_op jit(solution)/shard_map/lift/pallas_call | solution.py:389
  7.6 0.7 copy-done.17
  8.4 15.0 %exchange.4 = f32[16,24,256]{2,1,0:T(8,128)} custom-call(f32[16,24,256]{2,1,0:T(8,128)} %bitcast.30), custom_call_target="tpu_custom_call" | custom-call | tf_op jit(solution)/shard_map/exchange/pallas_call | solution.py:369
  23.3 1.3 copy-done.1
  24.6 1.0 copy-done.15
  25.6 3.2 %x_modes.1.ab_ref = f32[12,480,128]{2,1,0:T(8,128)S(1)} custom-call(f32[384,256]{1,0:T(8,128)S(1)} %bitcast.28, bf16[2,2,384,288]{3,2,1,0:T(8,128)(2,1)S(1)} %copy-done.1), custom_call_target="tpu_custom_call" | custom-call | tf_op jit(solution)/shard_map/x_modes/pallas_call | solution.py:391
  28.8 27.4 %mix.1.modes_ref = f32[12,12,24,20]{3,2,1,0:T(8,128)S(1)} custom-call(f32[69120,20]{1,0:T(8,128)} %bitcast.33, f32[12,480,128]{2,1,0:T(8,128)S(1)} %x_modes.1.ab_ref, bf16[40,480]{1,0:T(8,128)(2,1)S(1)} %copy-done.26), custom_call_target="tpu_custom_call" | custom-call | tf_op jit(solution)/shard_map/mix/pallas_call | solution.py:392
  56.3 0.9 x_rows.1
  57.3 0.7 copy-done.16
  58.0 15.0 %exchange.5 = f32[16,24,256]{2,1,0:T(8,128)} custom-call(f32[16,24,256]{2,1,0:T(8,128)} %bitcast.29), custom_call_target="tpu_custom_call" | custom-call | tf_op jit(solution)/shard_map/exchange/pallas_call | solution.py:369
  73.1 1.1 copy-done.7
  74.2 1.1 copy-done.11
  75.3 1.0 copy-done.13
  76.3 1.4 copy-done.18
  77.7 1.1 copy-done.19
  78.8 1.1 copy-done.20
  79.8 7.7 %middle.1 = (f32[320,512]{1,0:T(8,128)}, f32[320,512]{1,0:T(8,128)S(1)}, f32[384,256]{1,0:T(8,128)S(1)}) custom-call(f32[384,256]{1,0:T(8,128)S(1)} %bitcast.27, f32[320,512]{1,0:T(8,128)S(1)} %bitcast.24, f32[320,512]{1,0:T(8,128)S(1)} %bitcast.31, f32[20,20]{1,0:T(8,128)S(1)} %copy-done.25, bf16[320,20]{1,0:T(8,128)(2,1)S(1)} %copy-done.24, ...), custom_call_target="tpu_custom_call" | custom-call | tf_op jit(solution)/shard_map/middle/pallas_call | solution.py:401
  87.6 0.7 copy-done.22
  88.3 15.0 %exchange.6.rows_ref = f32[16,24,256]{2,1,0:T(8,128)} custom-call(f32[16,24,256]{2,1,0:T(8,128)} %bitcast.32), custom_call_target="tpu_custom_call" | custom-call | tf_op jit(solution)/shard_map/exchange/pallas_call | solution.py:369
  103.4 1.0 copy-done.9
  104.4 0.8 back_modes.1.back_ref
  105.2 33.1 %grads.1 = (f32[69120,20]{1,0:T(8,128)}, f32[12,480,128]{2,1,0:T(8,128)S(1)}) custom-call(f32[69120,20]{1,0:T(8,128)} %bitcast.34, f32[12,480,128]{2,1,0:T(8,128)} %copy-done, f32[12,12,24,20]{3,2,1,0:T(8,128)S(1)} %back_modes.1.back_ref), custom_call_target="tpu_custom_call" | custom-call | tf_op jit(solution)/shard_map/grads/pallas_call | solution.py:408
  138.3 1.6 %back_rows.1.rows_ref = f32[16,24,256]{2,1,0:T(8,128)S(1)} custom-call(f32[12,480,128]{2,1,0:T(8,128)S(1)} %get-tuple-element.12.sums_ref, bf16[2,2,384,288]{3,2,1,0:T(8,128)(2,1)S(1)} %copy-done.3, f32[16,24,256]{2,1,0:T(8,128)S(1)} %copy-done.9), custom_call_target="tpu_custom_call" | custom-call | tf_op jit(solution)/shard_map/back_rows/pallas_call | solution.py:414
  139.9 0.7 copy-done.14
  140.7 15.0 %exchange.7 = f32[16,24,256]{2,1,0:T(8,128)} custom-call(f32[16,24,256]{2,1,0:T(8,128)} %copy-done.14), custom_call_target="tpu_custom_call" | custom-call | tf_op jit(solution)/shard_map/exchange/pallas_call | solution.py:369
  155.7 1.0 copy-done.12
  156.7 3.7 %last.1 = f32[320,512]{1,0:T(8,128)} custom-call(f32[384,256]{1,0:T(8,128)S(1)} %bitcast.25, f32[320,512]{1,0:T(8,128)S(1)} %get-tuple-element.13.dpre_ref, f32[20,20]{1,0:T(8,128)S(1)} %copy-done.25, bf16[320,20]{1,0:T(8,128)(2,1)S(1)} %copy-done.24, bf16[2,2,384,512]{3,2,1,0:T(8,128)(2,1)S(1)} %copy-done.5, bf16[2,2,320,256]{3,2,1,0:T(8,128)(2,1)S(1)} %copy-done.8), custom_call_target="tpu_custom_call" | custom-call | tf_op jit(solution)/shard_map/last/pallas_call | solution.py:418
  161.2 0.6 slice_bitcast_fusion
  (44 shorter events, 1.0 us)
Async XLA Ops:
  1.5 1.4 copy-start.4
  2.9 1.1 copy-start.6
  4.0 1.1 copy-start.10
  7.6 0.7 copy-start.17
  23.3 1.3 copy-start.1
  24.6 1.0 copy-start.15
  25.6 3.2 %copy-start.26 = (bf16[40,480]{1,0:T(8,128)(2,1)S(1)}, bf16[40,480]{1,0:T(8,128)(2,1)}, u32[]{:S(2)}) copy-start(bf16[40,480]{1,0:T(8,128)(2,1)} %constant.23.clone.tile_ref) | copy-start | bytes 115204
  28.8 27.5 %copy-start = (f32[12,480,128]{2,1,0:T(8,128)}, f32[12,480,128]{2,1,0:T(8,128)S(1)}, u32[]{:S(2)}) copy-start(f32[12,480,128]{2,1,0:T(8,128)S(1)} %x_modes.1.ab_ref) | copy-start | bytes 8847364
  28.8 27.5 %copy-start.2 = (bf16[2,2,384,288]{3,2,1,0:T(8,128)(2,1)S(1)}, bf16[2,2,384,288]{3,2,1,0:T(8,128)(2,1)}, u32[]{:S(2)}) copy-start(bf16[2,2,384,288]{3,2,1,0:T(8,128)(2,1)} %constant.22.clone.x_ref) | copy-start | bytes 2654212
  56.3 16.8 %copy-start.23 = (bf16[2,320,256]{2,1,0:T(8,128)(2,1)S(1)}, bf16[2,320,256]{2,1,0:T(8,128)(2,1)}, u32[]{:S(2)}) copy-start(bf16[2,320,256]{2,1,0:T(8,128)(2,1)} %constant.26.clone.place_ref) | copy-start | bytes 983044
  56.3 16.8 %copy-start.24 = (bf16[320,20]{1,0:T(8,128)(2,1)S(1)}, bf16[320,20]{1,0:T(8,128)(2,1)}, u32[]{:S(2)}) copy-start(bf16[320,20]{1,0:T(8,128)(2,1)} %constant.24.clone.repeat_ref) | copy-start | bytes 38404
  56.3 16.8 %copy-start.25 = (f32[20,20]{1,0:T(8,128)S(1)}, f32[20,20]{1,0:T(8,128)}, u32[]{:S(2)}) copy-start(f32[20,20]{1,0:T(8,128)} %mix_ref.3) | copy-start | bytes 4804
  57.3 0.7 copy-start.16
  73.1 1.1 copy-start.7
  74.2 1.1 copy-start.11
  75.3 1.0 copy-start.13
  76.3 1.4 copy-start.18
  77.7 1.1 copy-start.19
  78.8 1.1 copy-start.20
  79.8 23.6 %copy-start.21 = (bf16[2,288,384]{2,1,0:T(8,128)(2,1)S(1)}, bf16[2,288,384]{2,1,0:T(8,128)(2,1)}, u32[]{:S(2)}) copy-start(bf16[2,288,384]{2,1,0:T(8,128)(2,1)} %constant.28.clone.x_ref) | copy-start | bytes 1327108
  87.6 0.7 copy-start.22
  103.4 1.0 copy-start.9
  105.2 33.1 %copy-start.3 = (bf16[2,2,384,288]{3,2,1,0:T(8,128)(2,1)S(1)}, bf16[2,2,384,288]{3,2,1,0:T(8,128)(2,1)}, u32[]{:S(2)}) copy-start(bf16[2,2,384,288]{3,2,1,0:T(8,128)(2,1)} %constant.22.clone.x_ref) | copy-start | bytes 2654212
  138.3 17.5 %copy-start.5 = (bf16[2,2,384,512]{3,2,1,0:T(8,128)(2,1)S(1)}, bf16[2,2,384,512]{3,2,1,0:T(8,128)(2,1)}, u32[]{:S(2)}) copy-start(bf16[2,2,384,512]{3,2,1,0:T(8,128)(2,1)} %constant.20.clone.depth_ref) | copy-start | bytes 4718596
  138.3 17.5 %copy-start.8 = (bf16[2,2,320,256]{3,2,1,0:T(8,128)(2,1)S(1)}, bf16[2,2,320,256]{3,2,1,0:T(8,128)(2,1)}, u32[]{:S(2)}) copy-start(bf16[2,2,320,256]{3,2,1,0:T(8,128)(2,1)} %constant.21.clone.y_ref) | copy-start | bytes 1966084
  139.9 0.7 copy-start.14
  155.7 1.0 copy-start.12
